TPU v7x, 256 devices: a whole 4x4x8 slice. The times are simulated.
256 devices in a mesh: dp: 32 (over y, z), tensor: 8 (over x, core).
Axes of the slice: x: 4, y: 4, z: 8, core: 2. Of those that a mesh axis runs over, the one named last changes fastest.
Arguments:
- query_residual: bfloat16 [2048, 4096], P('dp', 'tensor'), as said below
- query_hidden: bfloat16 [2048, 6144], P('dp', 'tensor'), may hold values from -6 to 6
- doc_residual: bfloat16 [4096, 4096], P('dp', 'tensor'), as said below
- doc_hidden: bfloat16 [4096, 6144], P('dp', 'tensor'), may hold values from -6 to 6
- down_weight: bfloat16 [6144, 4096], P('tensor'), may hold values from -0.078125 to 0.078125
- norm_gain: float32 [4096], replicated, may hold values from 0.5 to 2
- pos_index: int32 [2048], replicated, may hold values from 0 to 4095, as said below
- neg_index: int32 [2048], replicated, may hold values from 0 to 4095
Outputs:
- query_grad: bfloat16 [2048, 6144], P('dp', 'tensor')
- doc_grad: bfloat16 [4096, 6144], P('dp', 'tensor')
- loss: float32 [], replicated
Inputs may be any that keep to these rules, and one draw needn't show every extreme that they name: pos_index and neg_index together name every document exactly once. `query_residual`: entries of either sign. `doc_residual`: entries of either sign.
All inputs are finite; a program needn't handle non-finite values.
Results may differ from a plain program's by a relative error of at most 0.025.
Values may be sent and summed in bfloat16 or wider, within the bound.
A program may use at most 64 MiB of HBM per device.

v0:
```python
import jax
import jax.numpy as jnp
from jax import lax
from jax.sharding import PartitionSpec as P

EPS = 1e-06
TAU = 0.05
LOSS_SCALE = 256.0


def make_coef(scores, totals, sig, pos_hot, neg_hot):
    prob = jnp.exp(scores) / totals[:, None]
    mixed = prob - pos_hot * (1.0 + sig)[:, None] + neg_hot * sig[:, None]
    return (LOSS_SCALE / TAU * mixed).astype(jnp.bfloat16)


def shards(
    query_residual,
    query_hidden,
    doc_residual,
    doc_hidden,
    down_weight,
    norm_gain,
    pos_index,
    neg_index,
):
    queries = query_residual.shape[0]
    width = query_residual.shape[1]
    tensor_rank = lax.axis_index("tensor")
    dp_rank = lax.axis_index("dp")
    residual = jnp.concatenate([query_residual, doc_residual], 0).astype(jnp.float32)
    hidden = jnp.concatenate([query_hidden, doc_hidden], 0)
    projected = jnp.dot(hidden, down_weight, preferred_element_type=jnp.float32)
    gain_local = lax.dynamic_slice_in_dim(norm_gain, tensor_rank * width, width)
    outputs = lax.psum_scatter(projected, "tensor", scatter_dimension=1, tiled=True) + residual
    scaled = outputs * gain_local
    squares = lax.psum(jnp.sum(scaled * scaled, 1), "tensor")
    inverse = lax.rsqrt(squares + EPS)[:, None]
    unit = scaled * inverse
    embedded = unit.astype(jnp.bfloat16)
    q_emb = embedded[:queries]
    d_emb = embedded[queries:]
    all_docs = lax.all_gather(d_emb, "dp", axis=0, tiled=True)
    total_docs = all_docs.shape[0]
    partial_scores = lax.dot_general(
        q_emb, all_docs, (((1,), (1,)), ((), ())), preferred_element_type=jnp.float32
    )
    scores = lax.psum(partial_scores, "tensor") * (1.0 / TAU)
    totals = jnp.sum(jnp.exp(scores), 1)
    pos_local = lax.dynamic_slice_in_dim(pos_index, dp_rank * queries, queries)
    neg_local = lax.dynamic_slice_in_dim(neg_index, dp_rank * queries, queries)
    column = jnp.arange(total_docs, dtype=jnp.int32)
    pos_hot = (column[None, :] == pos_local[:, None]).astype(jnp.float32)
    neg_hot = (column[None, :] == neg_local[:, None]).astype(jnp.float32)
    s_pos = jnp.sum(scores * pos_hot, 1)
    s_neg = jnp.sum(scores * neg_hot, 1)
    margin = s_neg - s_pos
    sig = jax.nn.sigmoid(margin)
    loss_terms = jnp.log(totals) - s_pos + jax.nn.softplus(margin)
    all_queries = queries * lax.axis_size("dp")
    loss = lax.psum(jnp.sum(loss_terms), "dp") / all_queries
    coef = make_coef(scores, totals, sig, pos_hot, neg_hot)
    grad_q = jnp.dot(coef, all_docs, preferred_element_type=jnp.float32)
    grad_d = lax.psum_scatter(
        lax.dot_general(
            coef, q_emb, (((0,), (0,)), ((), ())), preferred_element_type=jnp.float32
        ).astype(jnp.bfloat16),
        "dp",
        scatter_dimension=0,
        tiled=True,
    ).astype(jnp.float32)
    grads = jnp.concatenate([grad_q, grad_d], 0)
    alignment = lax.psum(jnp.sum(unit * grads, 1), "tensor")
    grad_pre = (gain_local * ((grads - unit * alignment[:, None]) * inverse)).astype(jnp.bfloat16)
    back = lax.dot_general(
        lax.all_gather(grad_pre, "tensor", axis=1, tiled=True),
        down_weight,
        (((1,), (1,)), ((), ())),
        preferred_element_type=jnp.float32,
    )
    return (back[:queries].astype(jnp.bfloat16), back[queries:].astype(jnp.bfloat16), loss)


def solution(mesh):
    placed = (
        P("dp", "tensor"),
        P("dp", "tensor"),
        P("dp", "tensor"),
        P("dp", "tensor"),
        P("tensor", None),
        P(),
        P(),
        P(),
    )
    return jax.shard_map(
        shards,
        mesh=mesh,
        in_specs=placed,
        out_specs=(P("dp", "tensor"), P("dp", "tensor"), P()),
        check_vma=False,
    )
```

profile of v0, /device:TPU:0, one launch (start us, length us, event | category | flops | bytes accessed | tf_op | source)
XLA Modules:
  0.0 549.5 jit_solution(4800616251061774199)
XLA Ops:
  7.2 0.0 reduce-scatter.3.cloned.1.call-start
  7.2 6.1 %fusion = f32[192,4096]{1,0:T(8,128)} fusion(bf16[768,4096]{1,0:T(8,128)(2,1)} %param.12, bf16[128,768]{1,0:T(8,128)(2,1)} %param.11, bf16[64,768]{1,0:T(8,128)(2,1)} %param.9), kind=kOutput, calls=%fused_computation.14 | convolution fusion | flops 1208549376 | bytes 9732096 | tf_op jit(solution)/shard_map/dot_general | solution.py:33
  13.3 0.0 reduce-scatter.3.cloned.1.call-update
  13.3 0.0 all-gather.3.cloned.1.call-start
  13.4 0.8 dynamic_slice.9
  14.1 38.8 %reduce-scatter.3.cloned.1.call-done = f32[192,512]{1,0:T(8,128)} async-done(((f32[192,4096]{1,0:T(8,128)}), f32[192,512]{1,0:T(8,128)}) %reduce-scatter.3.cloned.1.call-update) | async-done | bytes 393232 | tf_op jit(solution)/shard_map/reduce_scatter | solution.py:35
  52.9 1.1 multiply_reduce_fusion.1
  54.1 13.1 %psum.28 = f32[192]{0:T(256)S(1)} all-reduce(f32[192]{0:T(256)S(1)} %multiply_reduce_fusion.1), channel_id=1, replica_groups=mesh['dp'=32,'tensor'=8] {'tensor'}, use_global_device_ids=true, to_apply=%region_2.0 | all-reduce | flops 192 | bytes 1536 | tf_op jit(solution)/shard_map/psum | solution.py:37
  67.2 1.1 multiply_convert_fusion.2
  68.3 0.7 slice.19
  69.0 0.0 all-reduce.2.cloned.1.call-start
  69.1 80.6 %all-gather.3.cloned.1.call-done = bf16[4096,512]{1,0:T(8,128)(2,1)} async-done(((bf16[128,512]{1,0:T(8,128)(2,1)}), bf16[4096,512]{1,0:T(8,128)(2,1)}) %all-gather.3.cloned.1.call-update) | async-done | bytes 4194320 | tf_op jit(solution)/shard_map/all_gather | solution.py:43
  149.6 4.5 fusion.5
  154.2 0.0 reduce-scatter.5.cloned.1.call-start
  154.2 0.8 dynamic_slice.10
  155.0 0.8 dynamic_slice.11
  155.8 63.2 %all-reduce.2.cloned.1.call-done = f32[64,4096]{1,0:T(8,128)} async-done(((f32[64,4096]{1,0:T(8,128)}), f32[64,4096]{1,0:T(8,128)}) %all-reduce.2.cloned.1.call-update) | async-done | bytes 1048592 | tf_op jit(solution)/shard_map/psum | solution.py:48
  219.0 1.8 exponential_reduce_fusion
  220.8 0.6 broadcast_add_fusion
  221.4 4.8 convolution_convert_fusion
  226.2 0.0 all-gather.5.cloned.1.call-start
  226.3 3.1 fusion.10
  229.4 217.7 %reduce-scatter.5.cloned.1.call-done = bf16[128,512]{1,0:T(8,128)(2,1)} async-done(((bf16[4096,512]{1,0:T(8,128)(2,1)}), bf16[128,512]{1,0:T(8,128)(2,1)}) %reduce-scatter.5.cloned.1.call-update) | async-done | bytes 131088 | tf_op jit(solution)/shard_map/reduce_scatter | solution.py:64
  447.0 0.9 convert_element_type.26
  448.0 0.2 multiply_reduce_fusion
  448.2 12.4 %psum.30 = f32[192]{0:T(256)S(1)} all-reduce(f32[192]{0:T(256)S(1)} %multiply_reduce_fusion), channel_id=1, replica_groups=mesh['dp'=32,'tensor'=8] {'tensor'}, use_global_device_ids=true, to_apply=%region_9.10 | all-reduce | flops 192 | bytes 1536 | tf_op jit(solution)/shard_map/psum | solution.py:73
  460.6 0.9 multiply_convert_fusion.1
  461.5 72.8 %psum.31 = f32[]{:T(128)} all-reduce(f32[]{:T(128)} %get-tuple-element.8), channel_id=1, replica_groups=mesh['dp'=32,'tensor'=8] {'dp'}, use_global_device_ids=true, to_apply=%region_11.12 | all-reduce | flops 1 | bytes 8 | tf_op jit(solution)/shard_map/psum | solution.py:61
  535.0 0.0 all-gather.5.cloned.1.call-done
  535.0 5.5 convolution_convert_fusion.1
  540.5 0.7 slice.21
  541.2 0.6 slice.20
  (13 shorter events, 0.1 us)
Async XLA Ops:
  7.2 45.8 %copy-start.1 = (bf16[128,512]{1,0:T(8,128)(2,1)S(1)}, bf16[128,512]{1,0:T(8,128)(2,1)}, u32[]{:S(2)}) copy-start(bf16[128,512]{1,0:T(8,128)(2,1)} %param.10) | copy-start | bytes 393220
  7.2 45.8 %copy-start.3 = (bf16[64,512]{1,0:T(8,128)(2,1)S(1)}, bf16[64,512]{1,0:T(8,128)(2,1)}, u32[]{:S(2)}) copy-start(bf16[64,512]{1,0:T(8,128)(2,1)} %param.8) | copy-start | bytes 196612
  7.2 45.8 %reduce-scatter.3.cloned.1.call-start = ((), (), s32[]{:S(2)}) async-start(), calls=%async_computation.2 | async-start | bytes 3538944 | tf_op jit(solution)/shard_map/reduce_scatter | solution.py:35
  13.3 136.3 %all-gather.3.cloned.1.call-start = ((), (), s32[]{:S(2)}) async-start(), calls=%async_computation.3 | async-start | bytes 4325376 | tf_op jit(solution)/shard_map/all_gather | solution.py:43
  69.0 150.0 %all-reduce.2.cloned.1.call-start = ((), (), s32[]{:S(2)}) async-start(), calls=%async_computation.4 | async-start | bytes 2097152 | tf_op jit(solution)/shard_map/psum | solution.py:48
  154.2 292.9 %reduce-scatter.5.cloned.1.call-start = ((), (), s32[]{:S(2)}) async-start(), calls=%async_computation.5 | async-start | bytes 4325376 | tf_op jit(solution)/shard_map/reduce_scatter | solution.py:64
  221.4 4.9 copy-start.2
  226.2 221.7 %copy-start = (f32[192,512]{1,0:T(8,128)S(1)}, f32[192,512]{1,0:T(8,128)}, u32[]{:S(2)}) copy-start(f32[192,512]{1,0:T(8,128)} %reduce-scatter.3.cloned.1.call-done) | copy-start | bytes 1179652
  226.2 308.7 %all-gather.5.cloned.1.call-start = ((), (), s32[]{:S(2)}) async-start(), calls=%async_computation.6 | async-start | bytes 1769472 | tf_op jit(solution)/shard_map/all_gather | solution.py:76
Sparse Core Ops, SparseCore 0:
  13.4 39.4 reduce-scatter.2
  69.1 80.4 all-gather.2
  154.3 64.6 all-reduce.1
  226.4 220.6 reduce-scatter.4
  461.6 22.8 all-gather.4
where the time goes:
time: 550 us; the launch traced here: 549 us
  waiting for transfers between devices  400 us (73%)
  blocking collectives  98.3 us (18%)
  matrix products  23.9 us (4%)
  between operations  15.7 us (3%)
  other arithmetic  6.64 us (1%)
    reduce_scatter x1, waiting for transfers between devices, shards(): lax.psum_scatter(lax.dot_general(coef, q_emb, (((0,), (0,)), ((), ())), p...  218 us
    all_gather x1, waiting for transfers between devices, shards(): all_docs = lax.all_gather(d_emb, 'dp', axis=0, tiled=True)  80.6 us
    psum x1, blocking collectives, shards(): loss = lax.psum(jnp.sum(loss_terms), 'dp') / all_queries  72.8 us
    psum x1, waiting for transfers between devices, shards(): scores = lax.psum(partial_scores, 'tensor') * (1.0 / TAU)  63.2 us
    reduce_scatter x1, waiting for transfers between devices, shards(): lax.psum_scatter(projected, 'tensor', scatter_dimension=1, tiled=True)  38.8 us
    psum x1, blocking collectives, shards(): squares = lax.psum(jnp.sum(scaled * scaled, 1), 'tensor')  13.1 us
    psum x1, blocking collectives, shards(): alignment = lax.psum(jnp.sum(unit * grads, 1), 'tensor')  12.4 us
  transfers between devices with their start and end apart: 5, of which 4 were waited for; matrix products, arithmetic and copies ran while one was open for 1% of the time, Pallas kernels for 0%

commit v1 on v0

v1 whole, which is shorter than its diff:
```python
import functools

import jax
import jax.numpy as jnp
from jax import lax
from jax.experimental import pallas as pl
from jax.experimental.pallas import tpu as pltpu
from jax.sharding import PartitionSpec as P

EPS = 1e-06
TAU = 0.05
LOSS_SCALE = 256.0
NX, NY, NZ = 4, 4, 8
NT = 2 * NX
MESH = pl.DeviceIdType.MESH
F32 = jnp.float32
BF16 = jnp.bfloat16


def dot_nn(a, b):
    return lax.dot_general(a, b, (((1,), (0,)), ((), ())), preferred_element_type=F32)


def dot_nt(a, b):
    return lax.dot_general(a, b, (((1,), (1,)), ((), ())), preferred_element_type=F32)


def eye(n, m, shift=0):
    rows = lax.broadcasted_iota(jnp.int32, (n, m), 0)
    cols = lax.broadcasted_iota(jnp.int32, (n, m), 1)
    return cols == rows + shift


def to_row(col):
    n = col.shape[0]
    return jnp.sum(jnp.where(eye(n, n), col, 0.0), axis=0, keepdims=True)


def to_col(row):
    n = row.shape[1]
    return jnp.sum(jnp.where(eye(n, n), row, 0.0), axis=1, keepdims=True)


def rows8(*rows):
    width = rows[0].shape[1]
    index = lax.broadcasted_iota(jnp.int32, (8, width), 0)
    out = jnp.zeros((8, width), F32)
    for i, row in enumerate(rows):
        out = jnp.where(index == i, row, out)
    return out


def pad_lanes(row, width):
    return jnp.concatenate([row, jnp.zeros((1, width - row.shape[1]), F32)], axis=1)


class Ids:
    def __init__(self):
        self.n = 0

    def take(self, n):
        base = self.n
        self.n += n
        return base


RID = Ids()
R_SIB, R_XQ, R_XD = RID.take(4), RID.take(4), RID.take(4)
R_ZQ, R_YD = RID.take(8), RID.take(4)
R_SSIB, R_SX = RID.take(4), RID.take(4)
R_STAT = RID.take(8)
R_CF = RID.take(8)
R_GQ, R_GD = RID.take(8), RID.take(4)
R_KD, R_KQ = RID.take(8), RID.take(8)
R_PD, R_PQ = RID.take(8), RID.take(8)
R_LOSS = RID.take(4)
N_SEND = 112
X_ORDER = (2, 1, 3)
Z_ORDER = (4, 3, 5, 2, 6, 1, 7)
Y_ORDER = (2, 1, 3)


def kernel(
    nq, nd, q_res, q_hid, d_res, d_hid, w_hbm, gain_ref, pos_ref, neg_ref,
    q_out, d_out, loss_out,
    hid, res, wv, s1, r1, s2, r2, acc, scf, qall, dall, sS, rS, s3, r3, stats,
    cf, ct, sq, rq, sd, rd, kd, kq, gp, ly, back, local, send, recv,
):
    dp = lax.axis_index("dp")
    t = lax.axis_index("tensor")
    x, c = t // 2, t % 2
    y, z = dp // NZ, dp % NZ

    def at_x(k):
        return (dp, 2 * ((x + k) % NX) + c)

    def at_t(k):
        return (dp, (t + k) % NT)

    def at_y(k):
        return (((y + k) % NY) * NZ + z, t)

    def at_z(k):
        return (y * NZ + (z + k) % NZ, t)

    sib = (dp, 2 * x + 1 - c)
    sends = []

    def push(src, dst, rid, device):
        copy = pltpu.make_async_remote_copy(
            src_ref=src, dst_ref=dst, send_sem=send.at[len(sends)], recv_sem=recv.at[rid],
            device_id=device, device_id_type=MESH,
        )
        copy.start()
        sends.append(copy)

    def got(dst, rid, device):
        pltpu.make_async_remote_copy(
            src_ref=dst, dst_ref=dst, send_sem=send.at[0], recv_sem=recv.at[rid],
            device_id=device, device_id_type=MESH,
        ).wait_recv()

    loads = []

    def load(src, dst):
        copy = pltpu.make_async_copy(src, dst, local.at[len(loads)])
        copy.start()
        loads.append(copy)
        return copy

    h_loads = [load(q_hid, hid.at[pl.ds(0, nq)]), load(d_hid, hid.at[pl.ds(nq, nd)])]
    x_all = X_ORDER + (0,)
    w_loads = {}
    width = res.shape[1]
    for a in (1, 0):
        for k in x_all:
            owner = 2 * ((x + k) % NX) + (c + a) % 2
            columns = pl.ds(pl.multiple_of(owner * width, width), width)
            w_loads[a, k] = load(w_hbm.at[:, columns], wv.at[4 * a + k])
    r_loads = [load(q_res, res.at[pl.ds(0, nq)]), load(d_res, res.at[pl.ds(nq, nd)])]

    barrier = pltpu.get_barrier_semaphore()
    peers = [at_t(k) for k in range(1, NT)] + [at_z(k) for k in range(1, NZ)]
    peers += [at_y(k) for k in range(1, NY)]
    for peer in peers:
        pl.semaphore_signal(barrier, inc=1, device_id=peer, device_id_type=MESH)

    for copy in h_loads:
        copy.wait()
    for i, k in enumerate(x_all):
        w_loads[1, k].wait()
        s1[k] = dot_nn(hid[...], wv[4 + k]).astype(BF16)
        if i == 0:
            pl.semaphore_wait(barrier, len(peers))
        push(s1.at[k], r1.at[k], R_SIB + k, sib)
    q_rows, d_rows = pl.ds(0, nq), pl.ds(nq, nd)
    for k in X_ORDER:
        w_loads[0, k].wait()
        part = dot_nn(hid[...], wv[k])
        got(r1.at[k], R_SIB + k, sib)
        s2[k - 1] = (part + r1[k].astype(F32)).astype(BF16)
        push(s2.at[k - 1, q_rows], r2.at[3 - k, q_rows], R_XQ + 4 - k, at_x(k))
    for k in X_ORDER:
        push(s2.at[k - 1, d_rows], r2.at[3 - k, d_rows], R_XD + 4 - k, at_x(k))
    w_loads[0, 0].wait()
    part = dot_nn(hid[...], wv[0])
    got(r1.at[0], R_SIB, sib)
    acc[...] = part + r1[0].astype(F32)
    for copy in r_loads:
        copy.wait()
    gain = gain_ref[t]

    for k in X_ORDER:
        got(r2.at[k - 1, q_rows], R_XQ + k, at_x(k))
    total = acc[0:nq] + res[0:nq].astype(F32)
    for k in (1, 2, 3):
        total = total + r2[k - 1, 0:nq].astype(F32)
    scaled = total * gain
    scf[0:nq] = scaled
    qall[z] = scaled.astype(BF16)
    for k in Z_ORDER:
        push(qall.at[z], qall.at[z], R_ZQ + 8 - k, at_z(k))
    for k in X_ORDER:
        got(r2.at[k - 1, d_rows], R_XD + k, at_x(k))
    total = acc[nq:] + res[nq:].astype(F32)
    for k in (1, 2, 3):
        total = total + r2[k - 1, nq:].astype(F32)
    scaled = total * gain
    scf[nq:] = scaled
    dall[y] = scaled.astype(BF16)
    for k in Y_ORDER:
        push(dall.at[y], dall.at[y], R_YD + 4 - k, at_y(k))
    own_ss_q = to_row(jnp.sum(scf[0:nq] * scf[0:nq], axis=1, keepdims=True))
    own_ss_d = to_row(jnp.sum(scf[nq:] * scf[nq:], axis=1, keepdims=True))

    for k in Y_ORDER:
        got(dall.at[(y + k) % NY], R_YD + k, at_y(k))
    all_d = NY * nd
    pieces = []
    for k in range(NY):
        rows = dall[k].astype(F32)
        pieces.append(to_row(jnp.sum(rows * rows, axis=1, keepdims=True)))
    ss_d = jnp.concatenate(pieces, axis=1)
    for k in Z_ORDER:
        got(qall.at[(z + k) % NZ], R_ZQ + k, at_z(k))

    def block(owner):
        rows = qall[owner]
        scores = dot_nt(rows, dall[...].reshape(all_d, width))
        wide = rows.astype(F32)
        ss_q = to_row(jnp.sum(wide * wide, axis=1, keepdims=True))
        return scores, rows8(pad_lanes(ss_q, all_d), ss_d)

    for k in x_all:
        scores, tail = block(2 * ((x + k) % NX) + 1 - c)
        sS[k, 0:nq] = scores
        sS[k, nq:] = tail
        push(sS.at[k], rS.at[k], R_SSIB + k, sib)
    for k in X_ORDER:
        scores, tail = block(2 * ((x + k) % NX) + c)
        got(rS.at[k], R_SSIB + k, sib)
        s3[k, 0:nq] = scores + rS[k, 0:nq]
        s3[k, nq:] = tail + rS[k, nq:]
        push(s3.at[k], r3.at[3 - k], R_SX + 4 - k, at_x(k))
    scores, tail = block(t)
    got(rS.at[0], R_SSIB, sib)
    s3[0, 0:nq] = scores + rS[0, 0:nq]
    s3[0, nq:] = tail + rS[0, nq:]
    for k in X_ORDER:
        got(r3.at[k - 1], R_SX + k, at_x(k))
    full = s3[0] + r3[0] + r3[1] + r3[2]

    inv_d = lax.rsqrt(full[nq + 1 : nq + 2] + EPS)
    inv_q = lax.rsqrt(to_col(full[nq : nq + 1, 0:nq]) + EPS)
    scores = full[0:nq] * inv_q * inv_d * (1.0 / TAU)
    expo = jnp.exp(scores)
    lanes = lax.broadcasted_iota(jnp.int32, (1, all_d), 1)
    column = ((lanes // nd) * NZ + z) * nd + lanes % nd
    group = (y * NZ + t) * nq
    row_at, shift = group // 128, group % 128
    pick = eye(nq, 128, shift)
    pos = jnp.sum(jnp.where(pick, pos_ref[row_at].astype(F32), 0.0), axis=1, keepdims=True)
    neg = jnp.sum(jnp.where(pick, neg_ref[row_at].astype(F32), 0.0), axis=1, keepdims=True)
    pos_hot = column == pos.astype(jnp.int32)
    neg_hot = column == neg.astype(jnp.int32)
    stats[z] = rows8(
        pad_lanes(to_row(jnp.sum(expo, axis=1, keepdims=True)), 128),
        pad_lanes(to_row(jnp.sum(jnp.where(pos_hot, scores, 0.0), axis=1, keepdims=True)), 128),
        pad_lanes(to_row(jnp.sum(jnp.where(neg_hot, scores, 0.0), axis=1, keepdims=True)), 128),
    )
    for k in Z_ORDER:
        push(stats.at[z], stats.at[z], R_STAT + 8 - k, at_z(k))
    for k in Z_ORDER:
        got(stats.at[(z + k) % NZ], R_STAT + k, at_z(k))
    stat = stats[0]
    for k in range(1, NZ):
        stat = stat + stats[k]
    tot_row, pos_row, neg_row = stat[0:1, 0:nq], stat[1:2, 0:nq], stat[2:3, 0:nq]
    margin = neg_row - pos_row
    soft = jnp.maximum(margin, 0.0) + jnp.log1p(jnp.exp(-jnp.abs(margin)))
    loss_part = jnp.sum(jnp.log(tot_row) - pos_row + soft, axis=1, keepdims=True)
    low = jnp.exp(-jnp.abs(margin))
    sig_row = jnp.where(margin >= 0.0, 1.0, low) / (1.0 + low)
    sig = to_col(sig_row)
    coef = expo / to_col(tot_row)
    coef = jnp.where(pos_hot, coef - (1.0 + sig), coef)
    coef = jnp.where(neg_hot, coef + sig, coef)
    cf[t] = ((LOSS_SCALE / TAU) * coef * inv_q * inv_d).astype(BF16)

    def gather_start(ref, rid):
        for k in X_ORDER:
            push(ref(t), ref(t), rid + 4 - k, at_x(k))
        push(ref(t), ref(t), rid, sib)

    def gather_pass(ref, rid):
        for k in X_ORDER:
            slot = ref(2 * ((x + k) % NX) + c)
            got(slot, rid + k, at_x(k))
            push(slot, slot, rid + 4 + k, sib)

    def gather_got(ref, rid, k):
        got(ref(2 * ((x + k) % NX) + 1 - c), rid + (4 + k if k else 0), sib)

    gather_start(lambda i: cf.at[i], R_CF)
    gather_pass(lambda i: cf.at[i], R_CF)
    for k in x_all:
        gather_got(lambda i: cf.at[i], R_CF, k)

    for k in Z_ORDER:
        sq[k - 1] = dot_nn(cf[(z + k) % NZ], dall[...].reshape(all_d, width)).astype(BF16)
        push(sq.at[k - 1], rq.at[7 - k], R_GQ + 8 - k, at_z(k))
    all_q = NZ * nq
    ct[...] = cf[...].reshape(all_q, all_d).T.reshape(NY, nd, all_q)
    for k in Y_ORDER:
        sd[k - 1] = dot_nn(ct[(y + k) % NY], qall[...].reshape(all_q, width)).astype(BF16)
        push(sd.at[k - 1], rd.at[3 - k], R_GD + 4 - k, at_y(k))
    grad_d = dot_nn(ct[y], qall[...].reshape(all_q, width))
    acc[0:nq] = dot_nn(cf[z], dall[...].reshape(all_d, width))

    def project_out(buffer, rid, raw, rows, own_ss, extra):
        kappa = to_row(jnp.sum(scf[rows] * raw, axis=1, keepdims=True))
        n = kappa.shape[1]
        tall = [kappa, own_ss] + extra
        buffer[t] = rows8(*[pad_lanes(r, 128) if r.shape[1] < 128 else r for r in tall])
        for k in range(1, NT):
            push(buffer.at[t], buffer.at[t], rid + 8 - k, at_t(k))
        for k in range(1, NT):
            got(buffer.at[(t + k) % NT], rid + k, at_t(k))
        summed = buffer[0]
        for k in range(1, NT):
            summed = summed + buffer[k]
        factor = to_col(summed[0:1, 0:n] / (summed[1:2, 0:n] + EPS))
        return (gain * (raw - scf[rows] * factor)).astype(BF16), summed

    for k in Y_ORDER:
        got(rd.at[k - 1], R_GD + k, at_y(k))
    for k in (1, 2, 3):
        grad_d = grad_d + rd[k - 1].astype(F32)
    loss_row = jnp.broadcast_to(loss_part, (1, 128))
    pre, summed = project_out(kd, R_KD, grad_d, slice(nq, nq + nd), own_ss_d, [loss_row])
    gp[t, nq:] = pre
    gather_start(lambda i: gp.at[i, d_rows], R_PD)
    ly[y] = summed
    for k in Y_ORDER:
        push(ly.at[y], ly.at[y], R_LOSS + 4 - k, at_y(k))

    for k in Z_ORDER:
        got(rq.at[k - 1], R_GQ + k, at_z(k))
    grad_q = acc[0:nq]
    for k in range(1, NZ):
        grad_q = grad_q + rq[k - 1].astype(F32)
    pre, _ = project_out(kq, R_KQ, grad_q, slice(0, nq), own_ss_q, [])
    gp[t, 0:nq] = pre
    gather_start(lambda i: gp.at[i, q_rows], R_PQ)

    gather_pass(lambda i: gp.at[i, d_rows], R_PD)
    gather_pass(lambda i: gp.at[i, q_rows], R_PQ)
    order = [(0, 0), (1, 0)] + [(a, k) for k in X_ORDER for a in (0, 1)]
    for rid, rows, out in ((R_PD, d_rows, d_out), (R_PQ, q_rows, q_out)):
        result = None
        for a, k in order:
            if a:
                gather_got(lambda i: gp.at[i, rows], rid, k)
            owner = 2 * ((x + k) % NX) + (c + a) % 2
            term = dot_nt(gp[owner, rows], wv[4 * a + k])
            result = term if result is None else result + term
        out[...] = result.astype(BF16)

    for k in Y_ORDER:
        got(ly.at[(y + k) % NY], R_LOSS + k, at_y(k))
    whole = ly[0] + ly[1] + ly[2] + ly[3]
    loss_out[0, 0] = jnp.sum(whole[2:3, 0:1]) * (1.0 / (NY * NZ * nq))
    for copy in sends:
        copy.wait_send()


def shards(
    query_residual, query_hidden, doc_residual, doc_hidden, down_weight, norm_gain, pos_index, neg_index,
):
    nq, width = query_residual.shape
    nd = doc_residual.shape[0]
    depth = query_hidden.shape[1]
    n = nq + nd
    all_q, all_d = NZ * nq, NY * nd
    anywhere = pl.BlockSpec(memory_space=pl.ANY)
    vmem = pl.BlockSpec(memory_space=pltpu.VMEM)
    query_grad, doc_grad, loss = pl.pallas_call(
        functools.partial(kernel, nq, nd),
        out_shape=(
            jax.ShapeDtypeStruct((nq, depth), BF16),
            jax.ShapeDtypeStruct((nd, depth), BF16),
            jax.ShapeDtypeStruct((1, 1), F32),
        ),
        in_specs=[anywhere] * 5 + [vmem] * 3,
        out_specs=(vmem, vmem, pl.BlockSpec(memory_space=pltpu.SMEM)),
        scratch_shapes=[
            pltpu.VMEM((n, depth), BF16),
            pltpu.VMEM((n, width), BF16),
            pltpu.VMEM((NT, depth, width), BF16),
            pltpu.VMEM((NX, n, width), BF16),
            pltpu.VMEM((NX, n, width), BF16),
            pltpu.VMEM((NX - 1, n, width), BF16),
            pltpu.VMEM((NX - 1, n, width), BF16),
            pltpu.VMEM((n, width), F32),
            pltpu.VMEM((n, width), F32),
            pltpu.VMEM((NZ, nq, width), BF16),
            pltpu.VMEM((NY, nd, width), BF16),
            pltpu.VMEM((NX, nq + 8, all_d), F32),
            pltpu.VMEM((NX, nq + 8, all_d), F32),
            pltpu.VMEM((NX, nq + 8, all_d), F32),
            pltpu.VMEM((NX - 1, nq + 8, all_d), F32),
            pltpu.VMEM((NZ, 8, 128), F32),
            pltpu.VMEM((NT, nq, all_d), BF16),
            pltpu.VMEM((NY, nd, all_q), BF16),
            pltpu.VMEM((NZ - 1, nq, width), BF16),
            pltpu.VMEM((NZ - 1, nq, width), BF16),
            pltpu.VMEM((NY - 1, nd, width), BF16),
            pltpu.VMEM((NY - 1, nd, width), BF16),
            pltpu.VMEM((NT, 8, 128), F32),
            pltpu.VMEM((NT, 8, 128), F32),
            pltpu.VMEM((NT, n, width), BF16),
            pltpu.VMEM((NY, 8, 128), F32),
            pltpu.VMEM((n, depth), F32),
            pltpu.SemaphoreType.DMA((12,)),
            pltpu.SemaphoreType.DMA((N_SEND,)),
            pltpu.SemaphoreType.DMA((RID.n,)),
        ],
        compiler_params=pltpu.CompilerParams(
            collective_id=0, has_side_effects=True, vmem_limit_bytes=48 * 2**20
        ),
        name="step",
    )(
        query_residual, query_hidden, doc_residual, doc_hidden, down_weight,
        norm_gain.reshape(NT, 1, width), pos_index.reshape(-1, 1, 128), neg_index.reshape(-1, 1, 128),
    )
    return query_grad, doc_grad, loss.reshape(())


def solution(mesh):
    placed = (
        P("dp", "tensor"),
        P("dp", "tensor"),
        P("dp", "tensor"),
        P("dp", "tensor"),
        P("tensor", None),
        P(),
        P(),
        P(),
    )
    return jax.shard_map(
        shards,
        mesh=mesh,
        in_specs=placed,
        out_specs=(P("dp", "tensor"), P("dp", "tensor"), P()),
        check_vma=False,
    )
```

time: 550 us -> 99.4 us (0.18)
  the two profiles are of different devices: /device:TPU:0 before, /device:TPU:1 now
where the time goes in v1:
time: 99.4 us; the launch traced here: 99 us
  Pallas kernels  89.7 us (90%)
  local copies, waits for them, and re-layouts  6.98 us (7%)
  between operations  2.35 us (2%)
    pallas_call x1, Pallas kernels, shards(): pl.pallas_call(functools.partial(kernel, nq, nd), out_shape=(jax.ShapeDty...  89.7 us
    unnamed x16, local copies, waits for them, and re-layouts  6.98 us

profile of v1, /device:TPU:1, one launch (start us, length us, event | category | flops | bytes accessed | tf_op | source)
XLA Modules:
  0.0 99.0 jit_solution(7041180969243119537)
XLA Ops:
  0.6 0.0 copy-start
  0.6 0.9 copy-done
  1.6 0.0 copy-start.1
  1.6 0.9 copy-done.1
  2.5 0.0 copy-start.2
  2.5 0.9 copy-done.2
  3.4 0.0 copy-start.3
  3.4 0.8 copy-done.3
  4.2 0.0 copy-start.4
  4.2 0.7 copy-done.4
  4.9 0.0 copy-start.5
  4.9 0.7 copy-done.5
  5.6 0.0 copy-start.6
  5.6 0.7 copy-done.6
  6.3 89.7 %step.1 = (bf16[64,768]{1,0:T(8,128)(2,1)S(1)}, bf16[128,768]{1,0:T(8,128)(2,1)S(1)}, f32[1,1]{1,0:T(1,128)}) custom-call(bf16[64,512]{1,0:T(8,128)(2,1)S(1)} %copy-done.3, bf16[64,768]{1,0:T(8,128)(2,1)S(1)} %copy-done.2, bf16[128,512]{1,0:T(8,128)(2,1)S(1)} %copy-done.1, bf16[128,768]{1,0:T(8,128)(2,1)S(1)} %copy-done, bf16[768,4096]{1,0:T(8,128)(2,1)} %w_hbm.1, ...), custom_call_target="tpu_custom_call" | custom-call | tf_op jit(solution)/shard_map/step/pallas_call | solution.py:367
  96.0 0.6 copy.14
  96.6 0.7 copy.15
Async XLA Ops:
  0.6 0.9 copy-start
  1.6 0.9 copy-start.1
  2.5 0.9 copy-start.2
  3.4 0.8 copy-start.3
  4.2 0.7 copy-start.4
  4.9 0.7 copy-start.5
  5.6 0.7 copy-start.6

commit v2 on v1

--- a/solution.py
+++ b/solution.py
@@ -66,14 +66,13 @@
 
 RID = Ids()
 R_SIB, R_XQ, R_XD = RID.take(4), RID.take(4), RID.take(4)
-R_ZQ, R_YD = RID.take(8), RID.take(4)
+R_ZQ, R_ZH, R_YD = RID.take(8), RID.take(1), RID.take(4)
 R_SSIB, R_SX = RID.take(4), RID.take(4)
 R_STAT = RID.take(8)
 R_CF = RID.take(8)
-R_GQ, R_GD = RID.take(8), RID.take(4)
-R_KD, R_KQ = RID.take(8), RID.take(8)
+R_G1, R_GH, R_GQ, R_GD = RID.take(2), RID.take(2), RID.take(8), RID.take(4)
+R_KZ, R_KT, R_KD, R_KY = RID.take(8), RID.take(8), RID.take(8), RID.take(4)
 R_PD, R_PQ = RID.take(8), RID.take(8)
-R_LOSS = RID.take(4)
 N_SEND = 112
 X_ORDER = (2, 1, 3)
 Z_ORDER = (4, 3, 5, 2, 6, 1, 7)
@@ -81,10 +80,10 @@
 
 
 def kernel(
-    nq, nd, q_res, q_hid, d_res, d_hid, w_hbm, gain_ref, pos_ref, neg_ref,
-    q_out, d_out, loss_out,
-    hid, res, wv, s1, r1, s2, r2, acc, scf, qall, dall, sS, rS, s3, r3, stats,
-    cf, ct, sq, rq, sd, rd, kd, kq, gp, ly, back, local, send, recv,
+    nq, nd, q_res, q_hid, d_res, d_hid, w_hbm, gain_hbm, pos_hbm, neg_hbm,
+    out, loss_out,
+    gain_ref, pos_ref, neg_ref, hid, res, wv, wt, s1, r1, s2, r2, acc, qall, dall, sS, rS, s3, r3, stats,
+    cf, ct, sq, hold, rq1, rqh, rq, sd, rd, kz, kt, kd, kds, ky, gp, local, send, recv,
 ):
     dp = lax.axis_index("dp")
     t = lax.axis_index("tensor")
@@ -119,6 +118,10 @@
             src_ref=dst, dst_ref=dst, send_sem=send.at[0], recv_sem=recv.at[rid],
             device_id=device, device_id_type=MESH,
         ).wait_recv()
+
+    def turn(first, last):
+        for i in range(first, last):
+            wt[i] = wv[i].T
 
     loads = []
 
@@ -137,7 +140,8 @@
             owner = 2 * ((x + k) % NX) + (c + a) % 2
             columns = pl.ds(pl.multiple_of(owner * width, width), width)
             w_loads[a, k] = load(w_hbm.at[:, columns], wv.at[4 * a + k])
-    r_loads = [load(q_res, res.at[pl.ds(0, nq)]), load(d_res, res.at[pl.ds(nq, nd)])]
+    r_loads = [load(gain_hbm, gain_ref), load(pos_hbm, pos_ref), load(neg_hbm, neg_ref)]
+    r_loads += [load(q_res, res.at[pl.ds(0, nq)]), load(d_res, res.at[pl.ds(nq, nd)])]
 
     barrier = pltpu.get_barrier_semaphore()
     peers = [at_t(k) for k in range(1, NT)] + [at_z(k) for k in range(1, NZ)]
@@ -175,23 +179,27 @@
     total = acc[0:nq] + res[0:nq].astype(F32)
     for k in (1, 2, 3):
         total = total + r2[k - 1, 0:nq].astype(F32)
-    scaled = total * gain
-    scf[0:nq] = scaled
-    qall[z] = scaled.astype(BF16)
-    for k in Z_ORDER:
+    qall[z] = (total * gain).astype(BF16)
+    for k in (2, 6, 1, 7):
         push(qall.at[z], qall.at[z], R_ZQ + 8 - k, at_z(k))
+    turn(0, 2)
     for k in X_ORDER:
         got(r2.at[k - 1, d_rows], R_XD + k, at_x(k))
     total = acc[nq:] + res[nq:].astype(F32)
     for k in (1, 2, 3):
         total = total + r2[k - 1, nq:].astype(F32)
-    scaled = total * gain
-    scf[nq:] = scaled
-    dall[y] = scaled.astype(BF16)
+    dall[y] = (total * gain).astype(BF16)
     for k in Y_ORDER:
         push(dall.at[y], dall.at[y], R_YD + 4 - k, at_y(k))
-    own_ss_q = to_row(jnp.sum(scf[0:nq] * scf[0:nq], axis=1, keepdims=True))
-    own_ss_d = to_row(jnp.sum(scf[nq:] * scf[nq:], axis=1, keepdims=True))
+    half = nq // 2
+    halves = {2: pl.ds(0, half), 6: pl.ds(half, half)}
+    for k in (2, 6):
+        slot = (z + k) % NZ
+        got(qall.at[slot], R_ZQ + k, at_z(k))
+        push(qall.at[slot], qall.at[slot], R_ZQ + (3 if k == 2 else 5), at_z(7 if k == 2 else 1))
+        part = qall.at[slot, halves[k]]
+        push(part, part, R_ZQ + 4 if k == 2 else R_ZH, at_z(8 - k))
+    turn(2, 4)
 
     for k in Y_ORDER:
         got(dall.at[(y + k) % NY], R_YD + k, at_y(k))
@@ -201,8 +209,11 @@
         rows = dall[k].astype(F32)
         pieces.append(to_row(jnp.sum(rows * rows, axis=1, keepdims=True)))
     ss_d = jnp.concatenate(pieces, axis=1)
-    for k in Z_ORDER:
+    for k in (1, 7, 3, 5):
         got(qall.at[(z + k) % NZ], R_ZQ + k, at_z(k))
+    slot = (z + 4) % NZ
+    got(qall.at[slot, halves[2]], R_ZQ + 4, at_z(2))
+    got(qall.at[slot, halves[6]], R_ZH, at_z(6))
 
     def block(owner):
         rows = qall[owner]
@@ -226,12 +237,14 @@
     got(rS.at[0], R_SSIB, sib)
     s3[0, 0:nq] = scores + rS[0, 0:nq]
     s3[0, nq:] = tail + rS[0, nq:]
+    turn(4, 6)
     for k in X_ORDER:
         got(r3.at[k - 1], R_SX + k, at_x(k))
     full = s3[0] + r3[0] + r3[1] + r3[2]
 
     inv_d = lax.rsqrt(full[nq + 1 : nq + 2] + EPS)
-    inv_q = lax.rsqrt(to_col(full[nq : nq + 1, 0:nq]) + EPS)
+    inv_q_row = lax.rsqrt(full[nq : nq + 1, 0:nq] + EPS)
+    inv_q = to_col(inv_q_row)
     scores = full[0:nq] * inv_q * inv_d * (1.0 / TAU)
     expo = jnp.exp(scores)
     lanes = lax.broadcasted_iota(jnp.int32, (1, all_d), 1)
@@ -250,6 +263,7 @@
     )
     for k in Z_ORDER:
         push(stats.at[z], stats.at[z], R_STAT + 8 - k, at_z(k))
+    turn(6, 8)
     for k in Z_ORDER:
         got(stats.at[(z + k) % NZ], R_STAT + k, at_z(k))
     stat = stats[0]
@@ -265,7 +279,8 @@
     coef = expo / to_col(tot_row)
     coef = jnp.where(pos_hot, coef - (1.0 + sig), coef)
     coef = jnp.where(neg_hot, coef + sig, coef)
-    cf[t] = ((LOSS_SCALE / TAU) * coef * inv_q * inv_d).astype(BF16)
+    coef = ((LOSS_SCALE / TAU) * coef * inv_q * inv_d).astype(BF16)
+    cf[t] = coef
 
     def gather_start(ref, rid):
         for k in X_ORDER:
@@ -282,74 +297,117 @@
         got(ref(2 * ((x + k) % NX) + 1 - c), rid + (4 + k if k else 0), sib)
 
     gather_start(lambda i: cf.at[i], R_CF)
+
+    inner = coef.astype(F32) * full[0:nq]
+    kz[z] = rows8(pad_lanes(to_row(jnp.sum(inner, axis=1, keepdims=True)), 128))
+    kd[t] = rows8(jnp.sum(inner, axis=0, keepdims=True), jnp.broadcast_to(loss_part, (1, all_d)))
+    for k in Z_ORDER:
+        push(kz.at[z], kz.at[z], R_KZ + 8 - k, at_z(k))
+    for k in range(1, NT):
+        push(kd.at[t], kd.at[t], R_KD + 8 - k, at_t(k))
     gather_pass(lambda i: cf.at[i], R_CF)
     for k in x_all:
         gather_got(lambda i: cf.at[i], R_CF, k)
 
-    for k in Z_ORDER:
-        sq[k - 1] = dot_nn(cf[(z + k) % NZ], dall[...].reshape(all_d, width)).astype(BF16)
-        push(sq.at[k - 1], rq.at[7 - k], R_GQ + 8 - k, at_z(k))
+    def grad_q(k):
+        return dot_nn(cf[(z + k) % NZ], dall[...].reshape(all_d, width))
+
+    for i, k in enumerate((3, 5)):
+        sq[i] = grad_q(k).astype(BF16)
+        push(sq.at[i], rq1.at[i], R_G1 + i, at_z(1 if k == 3 else 7))
+    sq[2] = grad_q(4).astype(BF16)
+    push(sq.at[2, halves[2]], rqh.at[0], R_GH, at_z(2))
+    push(sq.at[2, halves[6]], rqh.at[1], R_GH + 1, at_z(6))
+    for i, k in enumerate((1, 7)):
+        sq[3 + i] = grad_q(k).astype(BF16)
+        push(sq.at[3 + i], rq.at[1 - i], R_GQ + 8 - k, at_z(k))
+    for i, k in enumerate((2, 6)):
+        hold[i] = grad_q(k)
     all_q = NZ * nq
     ct[...] = cf[...].reshape(all_q, all_d).T.reshape(NY, nd, all_q)
     for k in Y_ORDER:
         sd[k - 1] = dot_nn(ct[(y + k) % NY], qall[...].reshape(all_q, width)).astype(BF16)
         push(sd.at[k - 1], rd.at[3 - k], R_GD + 4 - k, at_y(k))
+    for i, k in enumerate((2, 6)):
+        got(rq1.at[i], R_G1 + i, at_z(7 if k == 2 else 1))
+        got(rqh.at[i], R_GH + i, at_z(8 - k))
+        low = slice(0, half) if k == 2 else slice(half, nq)
+        high = slice(half, nq) if k == 2 else slice(0, half)
+        summed = hold[i] + rq1[i].astype(F32)
+        sq[5 + i, low] = (summed[low] + rqh[i].astype(F32)).astype(BF16)
+        sq[5 + i, high] = summed[high].astype(BF16)
+        push(sq.at[5 + i], rq.at[3 - i], R_GQ + 8 - k, at_z(k))
     grad_d = dot_nn(ct[y], qall[...].reshape(all_q, width))
-    acc[0:nq] = dot_nn(cf[z], dall[...].reshape(all_d, width))
-
-    def project_out(buffer, rid, raw, rows, own_ss, extra):
-        kappa = to_row(jnp.sum(scf[rows] * raw, axis=1, keepdims=True))
-        n = kappa.shape[1]
-        tall = [kappa, own_ss] + extra
-        buffer[t] = rows8(*[pad_lanes(r, 128) if r.shape[1] < 128 else r for r in tall])
-        for k in range(1, NT):
-            push(buffer.at[t], buffer.at[t], rid + 8 - k, at_t(k))
-        for k in range(1, NT):
-            got(buffer.at[(t + k) % NT], rid + k, at_t(k))
-        summed = buffer[0]
-        for k in range(1, NT):
-            summed = summed + buffer[k]
-        factor = to_col(summed[0:1, 0:n] / (summed[1:2, 0:n] + EPS))
-        return (gain * (raw - scf[rows] * factor)).astype(BF16), summed
+    acc[0:nq] = grad_q(0)
+
+    for k in range(1, NT):
+        got(kd.at[(t + k) % NT], R_KD + k, at_t(k))
+    summed = kd[0]
+    for k in range(1, NT):
+        summed = summed + kd[k]
+    summed = rows8(summed[0:1], summed[1:2], inv_d * inv_d)
+    for k in range(NY):
+        kds[k] = summed[:, k * nd : (k + 1) * nd]
+    for k in Y_ORDER:
+        push(kds.at[(y + k) % NY], ky.at[y], R_KY + 4 - k, at_y(k))
+    ky[y] = kds[y]
+    for k in Z_ORDER:
+        got(kz.at[(z + k) % NZ], R_KZ + k, at_z(k))
+    summed = kz[0]
+    for k in range(1, NZ):
+        summed = summed + kz[k]
+    kt[t] = rows8(pad_lanes(summed[0:1, 0:nq] * inv_q_row * inv_q_row, 128))
+    for k in range(1, NT):
+        push(kt.at[t], kt.at[t], R_KT + 8 - k, at_t(k))
 
     for k in Y_ORDER:
         got(rd.at[k - 1], R_GD + k, at_y(k))
     for k in (1, 2, 3):
         grad_d = grad_d + rd[k - 1].astype(F32)
-    loss_row = jnp.broadcast_to(loss_part, (1, 128))
-    pre, summed = project_out(kd, R_KD, grad_d, slice(nq, nq + nd), own_ss_d, [loss_row])
-    gp[t, nq:] = pre
+    for k in Y_ORDER:
+        got(ky.at[(y + k) % NY], R_KY + k, at_y(k))
+    summed = ky[0] + ky[1] + ky[2] + ky[3]
+    loss_out[0, 0] = jnp.sum(summed[1:2, 0:1]) * (1.0 / (NY * NZ * nq))
+    inverse2 = kds[y]
+    factor = to_col(summed[0:1] * inverse2[2:3])
+    gp[t, nq:] = (gain * (grad_d - dall[y].astype(F32) * factor)).astype(BF16)
     gather_start(lambda i: gp.at[i, d_rows], R_PD)
-    ly[y] = summed
-    for k in Y_ORDER:
-        push(ly.at[y], ly.at[y], R_LOSS + 4 - k, at_y(k))
-
-    for k in Z_ORDER:
-        got(rq.at[k - 1], R_GQ + k, at_z(k))
-    grad_q = acc[0:nq]
-    for k in range(1, NZ):
-        grad_q = grad_q + rq[k - 1].astype(F32)
-    pre, _ = project_out(kq, R_KQ, grad_q, slice(0, nq), own_ss_q, [])
-    gp[t, 0:nq] = pre
+
+    for i, k in enumerate((1, 7, 2, 6)):
+        got(rq.at[i], R_GQ + k, at_z(k))
+    for k in range(1, NT):
+        got(kt.at[(t + k) % NT], R_KT + k, at_t(k))
+    grad = acc[0:nq]
+    for i in range(4):
+        grad = grad + rq[i].astype(F32)
+    factor = kt[z]
+    factor = to_col(factor[0:1, 0:nq])
+    gp[t, 0:nq] = (gain * (grad - qall[z].astype(F32) * factor)).astype(BF16)
     gather_start(lambda i: gp.at[i, q_rows], R_PQ)
 
     gather_pass(lambda i: gp.at[i, d_rows], R_PD)
-    gather_pass(lambda i: gp.at[i, q_rows], R_PQ)
-    order = [(0, 0), (1, 0)] + [(a, k) for k in X_ORDER for a in (0, 1)]
-    for rid, rows, out in ((R_PD, d_rows, d_out), (R_PQ, q_rows, q_out)):
-        result = None
-        for a, k in order:
+    result = None
+    for a in (0, 1):
+        for k in (0,) + X_ORDER:
             if a:
-                gather_got(lambda i: gp.at[i, rows], rid, k)
+                gather_got(lambda i: gp.at[i, d_rows], R_PD, k)
             owner = 2 * ((x + k) % NX) + (c + a) % 2
-            term = dot_nt(gp[owner, rows], wv[4 * a + k])
+            term = dot_nn(gp[owner, nq:], wt[4 * a + k])
             result = term if result is None else result + term
-        out[...] = result.astype(BF16)
-
-    for k in Y_ORDER:
-        got(ly.at[(y + k) % NY], R_LOSS + k, at_y(k))
-    whole = ly[0] + ly[1] + ly[2] + ly[3]
-    loss_out[0, 0] = jnp.sum(whole[2:3, 0:1]) * (1.0 / (NY * NZ * nq))
+    out[nq:] = result.astype(BF16)
+    result = None
+    for a in (0, 1):
+        for k in (0,) + X_ORDER:
+            owner = 2 * ((x + k) % NX) + (c + a) % 2
+            if a:
+                gather_got(lambda i: gp.at[i, q_rows], R_PQ, k)
+            elif k:
+                slot = gp.at[owner, q_rows]
+                got(slot, R_PQ + k, at_x(k))
+                push(slot, slot, R_PQ + 4 + k, sib)
+            term = dot_nn(gp[owner, 0:nq], wt[4 * a + k])
+            result = term if result is None else result + term
+    out[0:nq] = result.astype(BF16)
     for copy in sends:
         copy.wait_send()
 
@@ -362,26 +420,25 @@
     depth = query_hidden.shape[1]
     n = nq + nd
     all_q, all_d = NZ * nq, NY * nd
-    anywhere = pl.BlockSpec(memory_space=pl.ANY)
+    hbm = pl.BlockSpec(memory_space=pltpu.HBM)
     vmem = pl.BlockSpec(memory_space=pltpu.VMEM)
-    query_grad, doc_grad, loss = pl.pallas_call(
+    grads, loss = pl.pallas_call(
         functools.partial(kernel, nq, nd),
-        out_shape=(
-            jax.ShapeDtypeStruct((nq, depth), BF16),
-            jax.ShapeDtypeStruct((nd, depth), BF16),
-            jax.ShapeDtypeStruct((1, 1), F32),
-        ),
-        in_specs=[anywhere] * 5 + [vmem] * 3,
-        out_specs=(vmem, vmem, pl.BlockSpec(memory_space=pltpu.SMEM)),
+        out_shape=(jax.ShapeDtypeStruct((n, depth), BF16), jax.ShapeDtypeStruct((1, 1), F32)),
+        in_specs=[hbm] * 8,
+        out_specs=(vmem, pl.BlockSpec(memory_space=pltpu.SMEM)),
         scratch_shapes=[
+            pltpu.VMEM((NT, 1, width), F32),
+            pltpu.VMEM((NZ * NY * nq // 128, 1, 128), jnp.int32),
+            pltpu.VMEM((NZ * NY * nq // 128, 1, 128), jnp.int32),
             pltpu.VMEM((n, depth), BF16),
             pltpu.VMEM((n, width), BF16),
             pltpu.VMEM((NT, depth, width), BF16),
+            pltpu.VMEM((NT, width, depth), BF16),
             pltpu.VMEM((NX, n, width), BF16),
             pltpu.VMEM((NX, n, width), BF16),
             pltpu.VMEM((NX - 1, n, width), BF16),
             pltpu.VMEM((NX - 1, n, width), BF16),
-            pltpu.VMEM((n, width), F32),
             pltpu.VMEM((n, width), F32),
             pltpu.VMEM((NZ, nq, width), BF16),
             pltpu.VMEM((NY, nd, width), BF16),
@@ -393,27 +450,31 @@
             pltpu.VMEM((NT, nq, all_d), BF16),
             pltpu.VMEM((NY, nd, all_q), BF16),
             pltpu.VMEM((NZ - 1, nq, width), BF16),
-            pltpu.VMEM((NZ - 1, nq, width), BF16),
+            pltpu.VMEM((2, nq, width), F32),
+            pltpu.VMEM((2, nq, width), BF16),
+            pltpu.VMEM((2, nq // 2, width), BF16),
+            pltpu.VMEM((4, nq, width), BF16),
             pltpu.VMEM((NY - 1, nd, width), BF16),
             pltpu.VMEM((NY - 1, nd, width), BF16),
+            pltpu.VMEM((NZ, 8, 128), F32),
             pltpu.VMEM((NT, 8, 128), F32),
-            pltpu.VMEM((NT, 8, 128), F32),
+            pltpu.VMEM((NT, 8, all_d), F32),
+            pltpu.VMEM((NY, 8, nd), F32),
+            pltpu.VMEM((NY, 8, nd), F32),
             pltpu.VMEM((NT, n, width), BF16),
-            pltpu.VMEM((NY, 8, 128), F32),
-            pltpu.VMEM((n, depth), F32),
-            pltpu.SemaphoreType.DMA((12,)),
+            pltpu.SemaphoreType.DMA((16,)),
             pltpu.SemaphoreType.DMA((N_SEND,)),
             pltpu.SemaphoreType.DMA((RID.n,)),
         ],
         compiler_params=pltpu.CompilerParams(
-            collective_id=0, has_side_effects=True, vmem_limit_bytes=48 * 2**20
+            collective_id=0, has_side_effects=True, vmem_limit_bytes=63 * 2**20
         ),
         name="step",
     )(
         query_residual, query_hidden, doc_residual, doc_hidden, down_weight,
         norm_gain.reshape(NT, 1, width), pos_index.reshape(-1, 1, 128), neg_index.reshape(-1, 1, 128),
     )
-    return query_grad, doc_grad, loss.reshape(())
+    return grads[:nq], grads[nq:], loss.reshape(())
 
 
 def solution(mesh):

time: 99.4 us -> 84.1 us (0.85)
  Pallas kernels: 89.7 us -> 78.4 us
  local copies, waits for them, and re-layouts: 6.98 us -> 3.16 us
    pallas_call x1, Pallas kernels: 89.7 us -> 78.4 us  [shards(): pl.pallas_call(functools.partial(kernel, nq, nd), out_shape=(jax.ShapeDty...]
    unnamed x16 -> x0, local copies, waits for them, and re-layouts: 6.98 us -> none
    slice x0 -> x2, local copies, waits for them, and re-layouts: none -> 3.16 us  [shards(): return (grads[:nq], grads[nq:], loss.reshape(()))]
where the time goes in v2:
time: 84.1 us; the launch traced here: 84 us
  Pallas kernels  78.4 us (93%)
  local copies, waits for them, and re-layouts  3.16 us (4%)
  between operations  2.46 us (3%)
    pallas_call x1, Pallas kernels, shards(): pl.pallas_call(functools.partial(kernel, nq, nd), out_shape=(jax.ShapeDty...  78.4 us
    slice x2, local copies, waits for them, and re-layouts, shards(): return (grads[:nq], grads[nq:], loss.reshape(()))  3.16 us

profile of v2, /device:TPU:1, one launch (start us, length us, event | category | flops | bytes accessed | tf_op | source)
XLA Modules:
  0.0 84.0 jit_solution(3233364122709654843)
XLA Ops:
  0.6 78.4 %step.1 = (bf16[192,768]{1,0:T(8,128)(2,1)}, f32[1,1]{1,0:T(1,128)}) custom-call(bf16[64,512]{1,0:T(8,128)(2,1)} %q_res.1, bf16[64,768]{1,0:T(8,128)(2,1)} %q_hid.1, bf16[128,512]{1,0:T(8,128)(2,1)} %d_res.1, bf16[128,768]{1,0:T(8,128)(2,1)} %d_hid.1, bf16[768,4096]{1,0:T(8,128)(2,1)} %w_hbm.1, f32[8,1,512]{2,1,0:T(1,128)} %bitcast.4, ...), custom_call_target="tpu_custom_call" | custom-call | tf_op jit(solution)/shard_map/step/pallas_call | solution.py:425
  79.0 1.5 %slice.6 = bf16[64,768]{1,0:T(8,128)(2,1)} slice(bf16[192,768]{1,0:T(8,128)(2,1)} %get-tuple-element.5), slice={[0:64], [0:768]} | slice | bytes 196608 | tf_op jit(solution)/shard_map/slice | solution.py:477
  80.5 1.6 %slice.7 = bf16[128,768]{1,0:T(8,128)(2,1)} slice(bf16[192,768]{1,0:T(8,128)(2,1)} %get-tuple-element.5), slice={[64:192], [0:768]} | slice | bytes 393216 | tf_op jit(solution)/shard_map/slice | solution.py:477

commit v3 on v2

--- a/solution.py
+++ b/solution.py
@@ -65,15 +65,17 @@
 
 
 RID = Ids()
-R_SIB, R_XQ, R_XD = RID.take(4), RID.take(4), RID.take(4)
-R_ZQ, R_ZH, R_YD = RID.take(8), RID.take(1), RID.take(4)
-R_SSIB, R_SX = RID.take(4), RID.take(4)
-R_STAT = RID.take(8)
+R_SQ, R_SD = RID.take(4), RID.take(4)
+R_XQ, R_XD = RID.take(4), (RID.take(4), RID.take(4))
+R_ZQ, R_ZH, R_QS = RID.take(8), RID.take(1), RID.take(8)
+R_YD, R_DS = (RID.take(4), RID.take(4)), (RID.take(4), RID.take(4))
+R_SX = RID.take(4)
+R_STAT, R_ROW = RID.take(8), RID.take(8)
 R_CF = RID.take(8)
 R_G1, R_GH, R_GQ, R_GD = RID.take(2), RID.take(2), RID.take(8), RID.take(4)
 R_KZ, R_KT, R_KD, R_KY = RID.take(8), RID.take(8), RID.take(8), RID.take(4)
 R_PD, R_PQ = RID.take(8), RID.take(8)
-N_SEND = 112
+N_SEND = 160
 X_ORDER = (2, 1, 3)
 Z_ORDER = (4, 3, 5, 2, 6, 1, 7)
 Y_ORDER = (2, 1, 3)
@@ -82,8 +84,8 @@
 def kernel(
     nq, nd, q_res, q_hid, d_res, d_hid, w_hbm, gain_hbm, pos_hbm, neg_hbm,
     out, loss_out,
-    gain_ref, pos_ref, neg_ref, hid, res, wv, wt, s1, r1, s2, r2, acc, qall, dall, sS, rS, s3, r3, stats,
-    cf, ct, sq, hold, rq1, rqh, rq, sd, rd, kz, kt, kd, kds, ky, gp, local, send, recv,
+    gain_ref, pos_ref, neg_ref, hid, res, wv, wt, s1, r1, s2, r2, acc, qall, qs, dall, ds, s3, r3, stats,
+    row, hot, cf, cg, ct, sq, hold, rq1, rqh, rq, sd, rd, kz, kt, kd, kds, ky, gp, local, send, recv,
 ):
     dp = lax.axis_index("dp")
     t = lax.axis_index("tensor")
@@ -151,46 +153,79 @@
 
     for copy in h_loads:
         copy.wait()
+    q_rows, d_rows = pl.ds(0, nq), pl.ds(nq, nd)
+    d_parts = [pl.ds(nq + i * (nd // 2), nd // 2) for i in range(2)]
     for i, k in enumerate(x_all):
         w_loads[1, k].wait()
-        s1[k] = dot_nn(hid[...], wv[4 + k]).astype(BF16)
+        s1[k, 0:nq] = dot_nn(hid[0:nq], wv[4 + k]).astype(BF16)
         if i == 0:
             pl.semaphore_wait(barrier, len(peers))
-        push(s1.at[k], r1.at[k], R_SIB + k, sib)
-    q_rows, d_rows = pl.ds(0, nq), pl.ds(nq, nd)
+        push(s1.at[k, q_rows], r1.at[k, q_rows], R_SQ + k, sib)
+    for k in x_all:
+        w_loads[0, k].wait()
+        part = dot_nn(hid[0:nq], wv[k])
+        got(r1.at[k, q_rows], R_SQ + k, sib)
+        part = part + r1[k, 0:nq].astype(F32)
+        if k:
+            s2[k - 1, 0:nq] = part.astype(BF16)
+            push(s2.at[k - 1, q_rows], r2.at[3 - k, q_rows], R_XQ + 4 - k, at_x(k))
+        else:
+            acc[0:nq] = part
+    for k in x_all:
+        s1[k, nq:] = dot_nn(hid[nq:], wv[4 + k]).astype(BF16)
+        push(s1.at[k, d_rows], r1.at[k, d_rows], R_SD + k, sib)
+    for k in x_all:
+        part = dot_nn(hid[nq:], wv[k])
+        got(r1.at[k, d_rows], R_SD + k, sib)
+        part = part + r1[k, nq:].astype(F32)
+        if k:
+            s2[k - 1, nq:] = part.astype(BF16)
+            push(s2.at[k - 1, d_parts[0]], r2.at[3 - k, d_parts[0]], R_XD[0] + 4 - k, at_x(k))
+        else:
+            acc[nq:] = part
     for k in X_ORDER:
-        w_loads[0, k].wait()
-        part = dot_nn(hid[...], wv[k])
-        got(r1.at[k], R_SIB + k, sib)
-        s2[k - 1] = (part + r1[k].astype(F32)).astype(BF16)
-        push(s2.at[k - 1, q_rows], r2.at[3 - k, q_rows], R_XQ + 4 - k, at_x(k))
-    for k in X_ORDER:
-        push(s2.at[k - 1, d_rows], r2.at[3 - k, d_rows], R_XD + 4 - k, at_x(k))
-    w_loads[0, 0].wait()
-    part = dot_nn(hid[...], wv[0])
-    got(r1.at[0], R_SIB, sib)
-    acc[...] = part + r1[0].astype(F32)
+        push(s2.at[k - 1, d_parts[1]], r2.at[3 - k, d_parts[1]], R_XD[1] + 4 - k, at_x(k))
     for copy in r_loads:
         copy.wait()
     gain = gain_ref[t]
 
+    parity = (z + c + 1) % 2
+    passed = []
+
+    def pass_q(k):
+        slot = (z + k) % NZ
+        copy = pltpu.make_async_remote_copy(
+            src_ref=qall.at[slot], dst_ref=qs.at[slot], send_sem=send.at[N_SEND - 8 + k],
+            recv_sem=recv.at[R_QS + k], device_id=sib, device_id_type=MESH,
+        )
+        passed.append((k, copy))
+
+        @pl.when(parity == k % 2)
+        def _():
+            copy.start()
+
+    def full_rows(rows):
+        total = acc[rows] + res[rows].astype(F32)
+        for k in (1, 2, 3):
+            total = total + r2[k - 1, rows].astype(F32)
+        return (total * gain).astype(BF16)
+
     for k in X_ORDER:
         got(r2.at[k - 1, q_rows], R_XQ + k, at_x(k))
-    total = acc[0:nq] + res[0:nq].astype(F32)
-    for k in (1, 2, 3):
-        total = total + r2[k - 1, 0:nq].astype(F32)
-    qall[z] = (total * gain).astype(BF16)
+    qall[z] = full_rows(slice(0, nq))
     for k in (2, 6, 1, 7):
         push(qall.at[z], qall.at[z], R_ZQ + 8 - k, at_z(k))
+    pass_q(0)
     turn(0, 2)
-    for k in X_ORDER:
-        got(r2.at[k - 1, d_rows], R_XD + k, at_x(k))
-    total = acc[nq:] + res[nq:].astype(F32)
-    for k in (1, 2, 3):
-        total = total + r2[k - 1, nq:].astype(F32)
-    dall[y] = (total * gain).astype(BF16)
-    for k in Y_ORDER:
-        push(dall.at[y], dall.at[y], R_YD + 4 - k, at_y(k))
+    for i in range(2):
+        for k in X_ORDER:
+            got(r2.at[k - 1, d_parts[i]], R_XD[i] + k, at_x(k))
+        low = i * (nd // 2)
+        dall[y, low : low + nd // 2] = full_rows(slice(nq + low, nq + low + nd // 2))
+        slot = dall.at[y, pl.ds(low, nd // 2)]
+        for k in Y_ORDER:
+            push(slot, slot, R_YD[i] + 4 - k, at_y(k))
+        push(slot, ds.at[y, pl.ds(low, nd // 2)], R_DS[i], sib)
     half = nq // 2
     halves = {2: pl.ds(0, half), 6: pl.ds(half, half)}
     for k in (2, 6):
@@ -199,44 +234,63 @@
         push(qall.at[slot], qall.at[slot], R_ZQ + (3 if k == 2 else 5), at_z(7 if k == 2 else 1))
         part = qall.at[slot, halves[k]]
         push(part, part, R_ZQ + 4 if k == 2 else R_ZH, at_z(8 - k))
+        pass_q(k)
+    for k in (1, 7):
+        got(qall.at[(z + k) % NZ], R_ZQ + k, at_z(k))
+        pass_q(k)
+    all_d = NY * nd
+    lanes = lax.broadcasted_iota(jnp.int32, (1, all_d), 1)
+    column = ((lanes // nd) * NZ + z) * nd + lanes % nd
+    for i in range(NZ):
+        at = y * (NZ * nq // 128) + i * nq // 128
+        pick = eye(nq, 128, i * nq % 128)
+        pos = jnp.sum(jnp.where(pick, pos_ref[at].astype(F32), 0.0), axis=1, keepdims=True)
+        neg = jnp.sum(jnp.where(pick, neg_ref[at].astype(F32), 0.0), axis=1, keepdims=True)
+        mark = jnp.where(column == neg.astype(jnp.int32), 2.0, 0.0)
+        hot[i] = jnp.where(column == pos.astype(jnp.int32), 1.0, mark)
     turn(2, 4)
 
-    for k in Y_ORDER:
-        got(dall.at[(y + k) % NY], R_YD + k, at_y(k))
-    all_d = NY * nd
-    pieces = []
-    for k in range(NY):
-        rows = dall[k].astype(F32)
-        pieces.append(to_row(jnp.sum(rows * rows, axis=1, keepdims=True)))
-    ss_d = jnp.concatenate(pieces, axis=1)
-    for k in (1, 7, 3, 5):
+    for i in range(2):
+        for k in Y_ORDER:
+            slot = (y + k) % NY
+            place = pl.ds(i * (nd // 2), nd // 2)
+            got(dall.at[slot, place], R_YD[i] + k, at_y(k))
+            push(dall.at[slot, place], ds.at[slot, place], R_DS[i] + k, sib)
+    for k in (3, 5):
         got(qall.at[(z + k) % NZ], R_ZQ + k, at_z(k))
+        pass_q(k)
     slot = (z + 4) % NZ
     got(qall.at[slot, halves[2]], R_ZQ + 4, at_z(2))
     got(qall.at[slot, halves[6]], R_ZH, at_z(6))
-
-    def block(owner):
-        rows = qall[owner]
+    pass_q(4)
+
+    for i in range(2):
+        for k in (0,) + Y_ORDER:
+            got(ds.at[(y + k) % NY, pl.ds(i * (nd // 2), nd // 2)], R_DS[i] + k, sib)
+
+    def squares(*blocks):
+        total = 0.0
+        for rows in blocks:
+            wide = rows.astype(F32)
+            total = total + wide * wide
+        return to_row(jnp.sum(total, axis=1, keepdims=True))
+
+    ss_d = jnp.concatenate([squares(dall[k], ds[k]) for k in range(NY)], axis=1)
+    for k in range(NZ):
+
+        @pl.when(parity != k % 2)
+        def _(k=k):
+            got(qs.at[(z + k) % NZ], R_QS + k, sib)
+
+    for k in x_all:
+        owner = 2 * ((x + k) % NX) + c
+        rows, other = qall[owner], qs[owner]
         scores = dot_nt(rows, dall[...].reshape(all_d, width))
-        wide = rows.astype(F32)
-        ss_q = to_row(jnp.sum(wide * wide, axis=1, keepdims=True))
-        return scores, rows8(pad_lanes(ss_q, all_d), ss_d)
-
-    for k in x_all:
-        scores, tail = block(2 * ((x + k) % NX) + 1 - c)
-        sS[k, 0:nq] = scores
-        sS[k, nq:] = tail
-        push(sS.at[k], rS.at[k], R_SSIB + k, sib)
-    for k in X_ORDER:
-        scores, tail = block(2 * ((x + k) % NX) + c)
-        got(rS.at[k], R_SSIB + k, sib)
-        s3[k, 0:nq] = scores + rS[k, 0:nq]
-        s3[k, nq:] = tail + rS[k, nq:]
-        push(s3.at[k], r3.at[3 - k], R_SX + 4 - k, at_x(k))
-    scores, tail = block(t)
-    got(rS.at[0], R_SSIB, sib)
-    s3[0, 0:nq] = scores + rS[0, 0:nq]
-    s3[0, nq:] = tail + rS[0, nq:]
+        scores = scores + dot_nt(other, ds[...].reshape(all_d, width))
+        s3[k, 0:nq] = scores
+        s3[k, nq:] = rows8(pad_lanes(squares(rows, other), all_d), ss_d)
+        if k:
+            push(s3.at[k], r3.at[3 - k], R_SX + 4 - k, at_x(k))
     turn(4, 6)
     for k in X_ORDER:
         got(r3.at[k - 1], R_SX + k, at_x(k))
@@ -247,22 +301,31 @@
     inv_q = to_col(inv_q_row)
     scores = full[0:nq] * inv_q * inv_d * (1.0 / TAU)
     expo = jnp.exp(scores)
-    lanes = lax.broadcasted_iota(jnp.int32, (1, all_d), 1)
-    column = ((lanes // nd) * NZ + z) * nd + lanes % nd
-    group = (y * NZ + t) * nq
-    row_at, shift = group // 128, group % 128
-    pick = eye(nq, 128, shift)
-    pos = jnp.sum(jnp.where(pick, pos_ref[row_at].astype(F32), 0.0), axis=1, keepdims=True)
-    neg = jnp.sum(jnp.where(pick, neg_ref[row_at].astype(F32), 0.0), axis=1, keepdims=True)
-    pos_hot = column == pos.astype(jnp.int32)
-    neg_hot = column == neg.astype(jnp.int32)
+    marks = hot[t]
+    pos_hot, neg_hot = marks == 1.0, marks == 2.0
     stats[z] = rows8(
         pad_lanes(to_row(jnp.sum(expo, axis=1, keepdims=True)), 128),
         pad_lanes(to_row(jnp.sum(jnp.where(pos_hot, scores, 0.0), axis=1, keepdims=True)), 128),
         pad_lanes(to_row(jnp.sum(jnp.where(neg_hot, scores, 0.0), axis=1, keepdims=True)), 128),
     )
+    def gather_start(ref, rid):
+        for k in X_ORDER:
+            push(ref(t), ref(t), rid + 4 - k, at_x(k))
+        push(ref(t), ref(t), rid, sib)
+
+    def gather_pass(ref, rid):
+        for k in X_ORDER:
+            slot = ref(2 * ((x + k) % NX) + c)
+            got(slot, rid + k, at_x(k))
+            push(slot, slot, rid + 4 + k, sib)
+
+    def gather_got(ref, rid, k):
+        got(ref(2 * ((x + k) % NX) + 1 - c), rid + (4 + k if k else 0), sib)
+
     for k in Z_ORDER:
         push(stats.at[z], stats.at[z], R_STAT + 8 - k, at_z(k))
+    cf[t] = (expo * inv_d).astype(BF16)
+    gather_start(lambda i: cf.at[i], R_CF)
     turn(6, 8)
     for k in Z_ORDER:
         got(stats.at[(z + k) % NZ], R_STAT + k, at_z(k))
@@ -271,46 +334,40 @@
         stat = stat + stats[k]
     tot_row, pos_row, neg_row = stat[0:1, 0:nq], stat[1:2, 0:nq], stat[2:3, 0:nq]
     margin = neg_row - pos_row
-    soft = jnp.maximum(margin, 0.0) + jnp.log1p(jnp.exp(-jnp.abs(margin)))
+    low = jnp.exp(-jnp.abs(margin))
+    sig = jnp.where(margin >= 0.0, 1.0, low) / (1.0 + low)
+    scale = (LOSS_SCALE / TAU) * inv_q_row
+    row[t] = rows8(
+        pad_lanes(scale / tot_row, 128),
+        pad_lanes(scale * (jnp.exp(pos_row) / tot_row - (1.0 + sig)), 128),
+        pad_lanes(scale * (jnp.exp(neg_row) / tot_row + sig), 128),
+    )
+    for k in range(1, NT):
+        push(row.at[t], row.at[t], R_ROW + 8 - k, at_t(k))
+    soft = jnp.maximum(margin, 0.0) + jnp.log1p(low)
     loss_part = jnp.sum(jnp.log(tot_row) - pos_row + soft, axis=1, keepdims=True)
-    low = jnp.exp(-jnp.abs(margin))
-    sig_row = jnp.where(margin >= 0.0, 1.0, low) / (1.0 + low)
-    sig = to_col(sig_row)
-    coef = expo / to_col(tot_row)
-    coef = jnp.where(pos_hot, coef - (1.0 + sig), coef)
-    coef = jnp.where(neg_hot, coef + sig, coef)
-    coef = ((LOSS_SCALE / TAU) * coef * inv_q * inv_d).astype(BF16)
-    cf[t] = coef
-
-    def gather_start(ref, rid):
-        for k in X_ORDER:
-            push(ref(t), ref(t), rid + 4 - k, at_x(k))
-        push(ref(t), ref(t), rid, sib)
-
-    def gather_pass(ref, rid):
-        for k in X_ORDER:
-            slot = ref(2 * ((x + k) % NX) + c)
-            got(slot, rid + k, at_x(k))
-            push(slot, slot, rid + 4 + k, sib)
-
-    def gather_got(ref, rid, k):
-        got(ref(2 * ((x + k) % NX) + 1 - c), rid + (4 + k if k else 0), sib)
-
-    gather_start(lambda i: cf.at[i], R_CF)
-
-    inner = coef.astype(F32) * full[0:nq]
+    gather_pass(lambda i: cf.at[i], R_CF)
+    for k in range(1, NT):
+        got(row.at[(t + k) % NT], R_ROW + k, at_t(k))
+    for k in x_all:
+        gather_got(lambda i: cf.at[i], R_CF, k)
+    for i in range(NT):
+        factors = row[i]
+        coef = cf[i].astype(F32) * to_col(factors[0:1, 0:nq])
+        marks = hot[i]
+        coef = jnp.where(marks == 1.0, to_col(factors[1:2, 0:nq]) * inv_d, coef)
+        coef = jnp.where(marks == 2.0, to_col(factors[2:3, 0:nq]) * inv_d, coef)
+        cg[i] = coef.astype(BF16)
+
+    inner = cg[t].astype(F32) * full[0:nq]
     kz[z] = rows8(pad_lanes(to_row(jnp.sum(inner, axis=1, keepdims=True)), 128))
     kd[t] = rows8(jnp.sum(inner, axis=0, keepdims=True), jnp.broadcast_to(loss_part, (1, all_d)))
     for k in Z_ORDER:
         push(kz.at[z], kz.at[z], R_KZ + 8 - k, at_z(k))
     for k in range(1, NT):
         push(kd.at[t], kd.at[t], R_KD + 8 - k, at_t(k))
-    gather_pass(lambda i: cf.at[i], R_CF)
-    for k in x_all:
-        gather_got(lambda i: cf.at[i], R_CF, k)
-
     def grad_q(k):
-        return dot_nn(cf[(z + k) % NZ], dall[...].reshape(all_d, width))
+        return dot_nn(cg[(z + k) % NZ], dall[...].reshape(all_d, width))
 
     for i, k in enumerate((3, 5)):
         sq[i] = grad_q(k).astype(BF16)
@@ -318,16 +375,16 @@
     sq[2] = grad_q(4).astype(BF16)
     push(sq.at[2, halves[2]], rqh.at[0], R_GH, at_z(2))
     push(sq.at[2, halves[6]], rqh.at[1], R_GH + 1, at_z(6))
+    all_q = NZ * nq
+    ct[...] = cg[...].reshape(all_q, all_d).T.reshape(NY, nd, all_q)
+    for k in Y_ORDER:
+        sd[k - 1] = dot_nn(ct[(y + k) % NY], qall[...].reshape(all_q, width)).astype(BF16)
+        push(sd.at[k - 1], rd.at[3 - k], R_GD + 4 - k, at_y(k))
     for i, k in enumerate((1, 7)):
         sq[3 + i] = grad_q(k).astype(BF16)
         push(sq.at[3 + i], rq.at[1 - i], R_GQ + 8 - k, at_z(k))
     for i, k in enumerate((2, 6)):
         hold[i] = grad_q(k)
-    all_q = NZ * nq
-    ct[...] = cf[...].reshape(all_q, all_d).T.reshape(NY, nd, all_q)
-    for k in Y_ORDER:
-        sd[k - 1] = dot_nn(ct[(y + k) % NY], qall[...].reshape(all_q, width)).astype(BF16)
-        push(sd.at[k - 1], rd.at[3 - k], R_GD + 4 - k, at_y(k))
     for i, k in enumerate((2, 6)):
         got(rq1.at[i], R_G1 + i, at_z(7 if k == 2 else 1))
         got(rqh.at[i], R_GH + i, at_z(8 - k))
@@ -410,6 +467,11 @@
     out[0:nq] = result.astype(BF16)
     for copy in sends:
         copy.wait_send()
+    for k, copy in passed:
+
+        @pl.when(parity == k % 2)
+        def _(copy=copy):
+            copy.wait_send()
 
 
 def shards(
@@ -424,7 +486,7 @@
     vmem = pl.BlockSpec(memory_space=pltpu.VMEM)
     grads, loss = pl.pallas_call(
         functools.partial(kernel, nq, nd),
-        out_shape=(jax.ShapeDtypeStruct((n, depth), BF16), jax.ShapeDtypeStruct((1, 1), F32)),
+        out_shape=(pltpu.VMEM((n, depth), BF16), jax.ShapeDtypeStruct((1, 1), F32)),
         in_specs=[hbm] * 8,
         out_specs=(vmem, pl.BlockSpec(memory_space=pltpu.SMEM)),
         scratch_shapes=[
@@ -441,12 +503,15 @@
             pltpu.VMEM((NX - 1, n, width), BF16),
             pltpu.VMEM((n, width), F32),
             pltpu.VMEM((NZ, nq, width), BF16),
+            pltpu.VMEM((NZ, nq, width), BF16),
             pltpu.VMEM((NY, nd, width), BF16),
-            pltpu.VMEM((NX, nq + 8, all_d), F32),
-            pltpu.VMEM((NX, nq + 8, all_d), F32),
+            pltpu.VMEM((NY, nd, width), BF16),
             pltpu.VMEM((NX, nq + 8, all_d), F32),
             pltpu.VMEM((NX - 1, nq + 8, all_d), F32),
             pltpu.VMEM((NZ, 8, 128), F32),
+            pltpu.VMEM((NT, 8, 128), F32),
+            pltpu.VMEM((NT, nq, all_d), F32),
+            pltpu.VMEM((NT, nq, all_d), BF16),
             pltpu.VMEM((NT, nq, all_d), BF16),
             pltpu.VMEM((NY, nd, all_q), BF16),
             pltpu.VMEM((NZ - 1, nq, width), BF16),
@@ -467,7 +532,7 @@
             pltpu.SemaphoreType.DMA((RID.n,)),
         ],
         compiler_params=pltpu.CompilerParams(
-            collective_id=0, has_side_effects=True, vmem_limit_bytes=63 * 2**20
+            collective_id=0, has_side_effects=True, vmem_limit_bytes=62 * 2**20
         ),
         name="step",
     )(

time: 84.1 us -> 78.3 us (0.931)
  Pallas kernels: 78.4 us -> 74.6 us
  local copies, waits for them, and re-layouts: 3.16 us -> 1.34 us
    pallas_call x1, Pallas kernels: 78.4 us -> 74.6 us  [shards(): pl.pallas_call(functools.partial(kernel, nq, nd), out_shape=(pltpu.VMEM((...]
    slice x2, local copies, waits for them, and re-layouts: 3.16 us -> 1.34 us  [shards(): return (grads[:nq], grads[nq:], loss.reshape(()))]
where the time goes in v3:
time: 78.3 us; the launch traced here: 78.2 us
  Pallas kernels  74.6 us (95%)
  between operations  2.33 us (3%)
  local copies, waits for them, and re-layouts  1.34 us (2%)
    pallas_call x1, Pallas kernels, shards(): pl.pallas_call(functools.partial(kernel, nq, nd), out_shape=(pltpu.VMEM((...  74.6 us

profile of v3, /device:TPU:1, one launch (start us, length us, event | category | flops | bytes accessed | tf_op | source)
XLA Modules:
  0.0 78.2 jit_solution(12787270805716208057)
XLA Ops:
  0.6 74.6 %step.1 = (bf16[192,768]{1,0:T(8,128)(2,1)S(1)}, f32[1,1]{1,0:T(1,128)}) custom-call(bf16[64,512]{1,0:T(8,128)(2,1)} %q_res.1, bf16[64,768]{1,0:T(8,128)(2,1)} %q_hid.1, bf16[128,512]{1,0:T(8,128)(2,1)} %d_res.1, bf16[128,768]{1,0:T(8,128)(2,1)} %d_hid.1, bf16[768,4096]{1,0:T(8,128)(2,1)} %w_hbm.1, f32[8,1,512]{2,1,0:T(1,128)} %bitcast.4, ...), custom_call_target="tpu_custom_call" | custom-call | tf_op jit(solution)/shard_map/step/pallas_call | solution.py:487
  75.2 0.6 slice.6
  75.8 0.7 slice.7

commit v4 on v3

v4 whole, which is shorter than its diff:
```python
import functools

import jax
import jax.numpy as jnp
from jax import lax
from jax.experimental import pallas as pl
from jax.experimental.pallas import tpu as pltpu
from jax.sharding import PartitionSpec as P

EPS = 1e-06
TAU = 0.05
LOSS_SCALE = 256.0
NX, NY, NZ = 4, 4, 8
NT = 2 * NX
MESH = pl.DeviceIdType.MESH
F32 = jnp.float32
BF16 = jnp.bfloat16


def dot_nn(a, b):
    return lax.dot_general(a, b, (((1,), (0,)), ((), ())), preferred_element_type=F32)


def dot_nt(a, b):
    return lax.dot_general(a, b, (((1,), (1,)), ((), ())), preferred_element_type=F32)


def eye(n, m, shift=0):
    rows = lax.broadcasted_iota(jnp.int32, (n, m), 0)
    cols = lax.broadcasted_iota(jnp.int32, (n, m), 1)
    return cols == rows + shift


def to_row(col):
    n = col.shape[0]
    return jnp.sum(jnp.where(eye(n, n), col, 0.0), axis=0, keepdims=True)


def to_col(row):
    n = row.shape[1]
    return jnp.sum(jnp.where(eye(n, n), row, 0.0), axis=1, keepdims=True)


def rows8(*rows):
    width = rows[0].shape[1]
    index = lax.broadcasted_iota(jnp.int32, (8, width), 0)
    out = jnp.zeros((8, width), F32)
    for i, row in enumerate(rows):
        out = jnp.where(index == i, row, out)
    return out


def pad_lanes(row, width):
    return jnp.concatenate([row, jnp.zeros((1, width - row.shape[1]), F32)], axis=1)


class Ids:
    def __init__(self):
        self.n = 0

    def take(self, n):
        base = self.n
        self.n += n
        return base


RID = Ids()
R_SIB = RID.take(4)
R_XQ, R_XD = RID.take(1), (RID.take(1), RID.take(1))
R_Z2, R_Z6, R_Z1, R_Z3, R_QS = (RID.take(1) for _ in range(5))
R_YD, R_DS = (RID.take(1), RID.take(1)), RID.take(1)
R_SX, R_SS = RID.take(1), RID.take(1)
R_STAT, R_ROW = RID.take(1), RID.take(1)
R_CF, R_CS = RID.take(4), RID.take(1)
R_G1, R_GH, R_GQ = RID.take(2), RID.take(2), RID.take(1)
R_GD = (RID.take(1), RID.take(1))
R_KZ, R_KT, R_KD, R_KY = (RID.take(1) for _ in range(4))
R_PD, R_PDS, R_PQ, R_PQS = (RID.take(1), RID.take(1)), RID.take(1), RID.take(4), RID.take(1)
X_ORDER = (2, 1, 3)
Z_ORDER = (4, 3, 5, 2, 6, 1, 7)
Y_ORDER = (2, 1, 3)


def kernel(
    nq, nd, q_res, q_hid, d_res, d_hid, w_hbm, gain_hbm, pos_hbm, neg_hbm,
    out, loss_out,
    gain_ref, pos_ref, neg_ref, hid, res, wv, wt, s1, r1, s2, r2, acc, qall, qs, dall, ds, s3, r3, s3t, r3t, stats,
    row, hot, cf, cg, ct, sq, hold, rq1, rqh, rq, sd, rd, kz, kt, kd, kds, ky, gp, local, send, recv,
):
    dp = lax.axis_index("dp")
    t = lax.axis_index("tensor")
    x, c = t // 2, t % 2
    y, z = dp // NZ, dp % NZ

    def at_x(k):
        return (dp, 2 * ((x + k) % NX) + c)

    def at_t(k):
        return (dp, (t + k) % NT)

    def at_y(k):
        return (((y + k) % NY) * NZ + z, t)

    def at_z(k):
        return (y * NZ + (z + k) % NZ, t)

    sib = (dp, 2 * x + 1 - c)
    sends = []

    def push(src, dst, rid, device):
        copy = pltpu.make_async_remote_copy(
            src_ref=src, dst_ref=dst, send_sem=send.at[0], recv_sem=recv.at[rid],
            device_id=device, device_id_type=MESH,
        )
        copy.start()
        sends.append(copy)

    def got(dst, rid, device):
        pltpu.make_async_remote_copy(
            src_ref=dst, dst_ref=dst, send_sem=send.at[0], recv_sem=recv.at[rid],
            device_id=device, device_id_type=MESH,
        ).wait_recv()

    def turn(first, last):
        for i in range(first, last):
            wt[i] = wv[i].T

    loads = []

    def load(src, dst):
        copy = pltpu.make_async_copy(src, dst, local.at[len(loads)])
        copy.start()
        loads.append(copy)
        return copy

    h_loads = [load(q_hid, hid.at[pl.ds(0, nq)]), load(d_hid, hid.at[pl.ds(nq, nd)])]
    x_all = X_ORDER + (0,)
    w_loads = {}
    width = res.shape[1]
    steps = ((1, 2), (1, 1), (0, 2), (1, 3), (0, 1), (1, 0), (0, 3), (0, 0))
    for a, k in steps:
        owner = 2 * ((x + k) % NX) + (c + a) % 2
        columns = pl.ds(pl.multiple_of(owner * width, width), width)
        w_loads[a, k] = load(w_hbm.at[:, columns], wv.at[4 * a + k])
    r_loads = [load(gain_hbm, gain_ref), load(pos_hbm, pos_ref), load(neg_hbm, neg_ref)]
    r_loads += [load(q_res, res.at[pl.ds(0, nq)]), load(d_res, res.at[pl.ds(nq, nd)])]

    barrier = pltpu.get_barrier_semaphore()
    peers = [at_t(k) for k in range(1, NT)] + [at_z(k) for k in range(1, NZ)]
    peers += [at_y(k) for k in range(1, NY)]
    for peer in peers:
        pl.semaphore_signal(barrier, inc=1, device_id=peer, device_id_type=MESH)

    for copy in h_loads:
        copy.wait()
    q_rows, d_rows = pl.ds(0, nq), pl.ds(nq, nd)
    d_parts = [pl.ds(nq + i * (nd // 2), nd // 2) for i in range(2)]
    for i, (a, k) in enumerate(steps):
        w_loads[a, k].wait()
        part = dot_nn(hid[...], wv[4 * a + k])
        if a:
            s1[k] = part.astype(BF16)
            if i == 0:
                pl.semaphore_wait(barrier, len(peers))
            push(s1.at[k], r1.at[k], R_SIB + k, sib)
            continue
        got(r1.at[k], R_SIB + k, sib)
        part = part + r1[k].astype(F32)
        if k:
            s2[k - 1] = part.astype(BF16)
            push(s2.at[k - 1, q_rows], r2.at[3 - k, q_rows], R_XQ, at_x(k))
            push(s2.at[k - 1, d_parts[0]], r2.at[3 - k, d_parts[0]], R_XD[0], at_x(k))
        else:
            acc[...] = part
        if k == 3:
            for k in X_ORDER:
                push(s2.at[k - 1, d_parts[1]], r2.at[3 - k, d_parts[1]], R_XD[1], at_x(k))
    for copy in r_loads:
        copy.wait()
    gain = gain_ref[t]

    parity = (z + c + 1) % 2
    passed = []

    def pass_q(k):
        slot = (z + k) % NZ
        copy = pltpu.make_async_remote_copy(
            src_ref=qall.at[slot], dst_ref=qs.at[slot], send_sem=send.at[0],
            recv_sem=recv.at[R_QS], device_id=sib, device_id_type=MESH,
        )
        passed.append((k, copy))

        @pl.when(parity == k % 2)
        def _():
            copy.start()

    def full_rows(rows):
        total = acc[rows] + res[rows].astype(F32)
        for k in (1, 2, 3):
            total = total + r2[k - 1, rows].astype(F32)
        return (total * gain).astype(BF16)

    got(r2.at[:, q_rows], R_XQ, sib)
    qall[z] = full_rows(slice(0, nq))
    for k in (2, 6, 1, 7):
        push(qall.at[z], qall.at[z], {2: R_Z6, 6: R_Z2}.get(k, R_Z1), at_z(k))
    pass_q(0)
    turn(0, 2)
    for i in range(2):
        got(r2.at[:, d_parts[i]], R_XD[i], sib)
        low = i * (nd // 2)
        dall[y, low : low + nd // 2] = full_rows(slice(nq + low, nq + low + nd // 2))
        slot = dall.at[y, pl.ds(low, nd // 2)]
        for k in Y_ORDER:
            push(slot, slot, R_YD[i], at_y(k))
        push(slot, ds.at[y, pl.ds(low, nd // 2)], R_DS, sib)
    half = nq // 2
    halves = {2: pl.ds(0, half), 6: pl.ds(half, half)}
    for k in (2, 6):
        slot = (z + k) % NZ
        got(qall.at[slot], R_Z2 if k == 2 else R_Z6, at_z(k))
        push(qall.at[slot], qall.at[slot], R_Z3, at_z(7 if k == 2 else 1))
        part = qall.at[slot, halves[k]]
        push(part, part, R_Z3, at_z(8 - k))
        pass_q(k)
    got(qall.at[pl.ds(0, 2)], R_Z1, sib)
    pass_q(1)
    pass_q(7)
    all_d = NY * nd
    lanes = lax.broadcasted_iota(jnp.int32, (1, all_d), 1)
    column = ((lanes // nd) * NZ + z) * nd + lanes % nd
    for i in range(NZ):
        at = y * (NZ * nq // 128) + i * nq // 128
        pick = eye(nq, 128, i * nq % 128)
        pos = jnp.sum(jnp.where(pick, pos_ref[at].astype(F32), 0.0), axis=1, keepdims=True)
        neg = jnp.sum(jnp.where(pick, neg_ref[at].astype(F32), 0.0), axis=1, keepdims=True)
        mark = jnp.where(column == neg.astype(jnp.int32), 2.0, 0.0)
        hot[i] = jnp.where(column == pos.astype(jnp.int32), 1.0, mark)
    turn(2, 4)

    for i in range(2):
        place = pl.ds(i * (nd // 2), nd // 2)
        got(dall.at[pl.ds(0, 3), place], R_YD[i], sib)
        for k in Y_ORDER:
            slot = (y + k) % NY
            push(dall.at[slot, place], ds.at[slot, place], R_DS, sib)
    got(qall.at[pl.ds(0, 3)], R_Z3, sib)
    for k in (3, 5, 4):
        pass_q(k)

    got(ds, R_DS, sib)

    def squares(*blocks):
        total = 0.0
        for rows in blocks:
            wide = rows.astype(F32)
            total = total + wide * wide
        return to_row(jnp.sum(total, axis=1, keepdims=True))

    ss_d = jnp.concatenate([squares(dall[k], ds[k]) for k in range(NY)], axis=1)
    got(qs.at[pl.ds(0, NZ // 2)], R_QS, sib)
    owners = [2 * ((x + k) % NX) + c for k in x_all]
    for k, owner in zip(x_all, owners):
        s3t[k] = rows8(pad_lanes(squares(qall[owner], qs[owner]), all_d), ss_d)
        if k:
            push(s3t.at[k], r3t.at[3 - k], R_SS, at_x(k))
    scores = dot_nt(jnp.concatenate([qall[i] for i in owners], 0), dall[...].reshape(all_d, width))
    scores = scores + dot_nt(jnp.concatenate([qs[i] for i in owners], 0), ds[...].reshape(all_d, width))
    for i, k in enumerate(X_ORDER):
        s3[k - 1] = scores[i * nq : (i + 1) * nq].astype(BF16)
        push(s3.at[k - 1], r3.at[3 - k], R_SX, at_x(k))
    own_scores = scores[3 * nq :]
    turn(4, 6)
    got(r3t, R_SS, sib)
    tail = s3t[0] + r3t[0] + r3t[1] + r3t[2]
    inv_d = lax.rsqrt(tail[1:2] + EPS)
    inv_q_row = lax.rsqrt(tail[0:1, 0:nq] + EPS)
    inv_q = to_col(inv_q_row)
    got(r3, R_SX, sib)
    full = own_scores
    for k in (1, 2, 3):
        full = full + r3[k - 1].astype(F32)

    scores = full * inv_q * inv_d * (1.0 / TAU)
    expo = jnp.exp(scores)
    marks = hot[t]
    pos_hot, neg_hot = marks == 1.0, marks == 2.0
    stats[z] = rows8(
        pad_lanes(to_row(jnp.sum(expo, axis=1, keepdims=True)), 128),
        pad_lanes(to_row(jnp.sum(jnp.where(pos_hot, scores, 0.0), axis=1, keepdims=True)), 128),
        pad_lanes(to_row(jnp.sum(jnp.where(neg_hot, scores, 0.0), axis=1, keepdims=True)), 128),
    )
    def gather_start(ref, rid, pass_rid, each=1):
        for k in X_ORDER:
            push(ref(t), ref(t), rid + each * (4 - k), at_x(k))
        push(ref(t), ref(t), pass_rid, sib)

    def gather_pass(ref, pass_rid, k):
        slot = ref(2 * ((x + k) % NX) + c)
        push(slot, slot, pass_rid, sib)

    for k in Z_ORDER:
        push(stats.at[z], stats.at[z], R_STAT, at_z(k))
    cf[t] = (expo * inv_d).astype(BF16)
    gather_start(lambda i: cf.at[i], R_CF, R_CS)
    turn(6, 8)
    got(stats.at[pl.ds(0, NZ - 1)], R_STAT, sib)
    stat = stats[0]
    for k in range(1, NZ):
        stat = stat + stats[k]
    tot_row, pos_row, neg_row = stat[0:1, 0:nq], stat[1:2, 0:nq], stat[2:3, 0:nq]
    margin = neg_row - pos_row
    low = jnp.exp(-jnp.abs(margin))
    sig = jnp.where(margin >= 0.0, 1.0, low) / (1.0 + low)
    scale = (LOSS_SCALE / TAU) * inv_q_row
    row[t] = rows8(
        pad_lanes(scale / tot_row, 128),
        pad_lanes(scale * (jnp.exp(pos_row) / tot_row - (1.0 + sig)), 128),
        pad_lanes(scale * (jnp.exp(neg_row) / tot_row + sig), 128),
    )
    for k in range(1, NT):
        push(row.at[t], row.at[t], R_ROW, at_t(k))
    soft = jnp.maximum(margin, 0.0) + jnp.log1p(low)
    loss_part = jnp.sum(jnp.log(tot_row) - pos_row + soft, axis=1, keepdims=True)
    for k in X_ORDER:
        got(cf.at[2 * ((x + k) % NX) + c], R_CF + k, at_x(k))
        gather_pass(lambda i: cf.at[i], R_CS, k)
    got(row.at[pl.ds(0, NT - 1)], R_ROW, sib)
    got(cf.at[pl.ds(0, NX)], R_CS, sib)
    for i in range(NT):
        factors = row[i]
        coef = cf[i].astype(F32) * to_col(factors[0:1, 0:nq])
        marks = hot[i]
        coef = jnp.where(marks == 1.0, to_col(factors[1:2, 0:nq]) * inv_d, coef)
        coef = jnp.where(marks == 2.0, to_col(factors[2:3, 0:nq]) * inv_d, coef)
        cg[i] = coef.astype(BF16)

    inner = cg[t].astype(F32) * full
    kz[z] = rows8(pad_lanes(to_row(jnp.sum(inner, axis=1, keepdims=True)), 128))
    kd[t] = rows8(jnp.sum(inner, axis=0, keepdims=True), jnp.broadcast_to(loss_part, (1, all_d)))
    for k in Z_ORDER:
        push(kz.at[z], kz.at[z], R_KZ, at_z(k))
    for k in range(1, NT):
        push(kd.at[t], kd.at[t], R_KD, at_t(k))
    def grad_q(*offsets):
        rows = [cg[(z + k) % NZ] for k in offsets]
        grad = dot_nn(jnp.concatenate(rows, 0), dall[...].reshape(all_d, width))
        return [grad[i * nq : (i + 1) * nq] for i in range(len(offsets))]

    for i, grad in enumerate(grad_q(3, 5, 4)):
        sq[i] = grad.astype(BF16)
    for i, k in enumerate((3, 5)):
        push(sq.at[i], rq1.at[i], R_G1 + i, at_z(1 if k == 3 else 7))
    push(sq.at[2, halves[2]], rqh.at[0], R_GH, at_z(2))
    push(sq.at[2, halves[6]], rqh.at[1], R_GH + 1, at_z(6))
    all_q = NZ * nq
    ct[...] = cg[...].reshape(all_q, all_d).T.reshape(NY, nd, all_q)
    rows = jnp.concatenate([ct[(y + k) % NY] for k in Y_ORDER + (0,)], 0)
    grad = dot_nn(rows, qall[...].reshape(all_q, width))
    d_halves = [pl.ds(i * (nd // 2), nd // 2) for i in range(2)]
    for i, k in enumerate(Y_ORDER):
        sd[k - 1] = grad[i * nd : (i + 1) * nd].astype(BF16)
    acc[nq:] = grad[3 * nd :]
    for half_at, rid in zip(d_halves, R_GD):
        for k in Y_ORDER:
            push(sd.at[k - 1, half_at], rd.at[3 - k, half_at], rid, at_y(k))
    first, second, third, fourth, own = grad_q(1, 7, 2, 6, 0)
    sq[3], sq[4] = first.astype(BF16), second.astype(BF16)
    for i, k in enumerate((1, 7)):
        push(sq.at[3 + i], rq.at[1 - i], R_GQ, at_z(k))
    hold[0], hold[1] = third, fourth
    acc[0:nq] = own
    got(kd.at[pl.ds(0, NT - 1)], R_KD, sib)
    summed = kd[0]
    for k in range(1, NT):
        summed = summed + kd[k]
    summed = rows8(summed[0:1], summed[1:2], inv_d * inv_d)
    for k in range(NY):
        kds[k] = summed[:, k * nd : (k + 1) * nd]
    for k in Y_ORDER:
        push(kds.at[(y + k) % NY], ky.at[y], R_KY, at_y(k))
    ky[y] = kds[y]
    for i, k in enumerate((2, 6)):
        got(rq1.at[i], R_G1 + i, at_z(7 if k == 2 else 1))
        got(rqh.at[i], R_GH + i, at_z(8 - k))
        low = slice(0, half) if k == 2 else slice(half, nq)
        high = slice(half, nq) if k == 2 else slice(0, half)
        summed = hold[i] + rq1[i].astype(F32)
        sq[5 + i, low] = (summed[low] + rqh[i].astype(F32)).astype(BF16)
        sq[5 + i, high] = summed[high].astype(BF16)
        push(sq.at[5 + i], rq.at[3 - i], R_GQ, at_z(k))
    got(kz.at[pl.ds(0, NZ - 1)], R_KZ, sib)
    summed = kz[0]
    for k in range(1, NZ):
        summed = summed + kz[k]
    kt[t] = rows8(pad_lanes(summed[0:1, 0:nq] * inv_q_row * inv_q_row, 128))
    for k in range(1, NT):
        push(kt.at[t], kt.at[t], R_KT, at_t(k))

    got(ky.at[pl.ds(0, NY - 1)], R_KY, sib)
    summed = ky[0] + ky[1] + ky[2] + ky[3]
    loss_out[0, 0] = jnp.sum(summed[1:2, 0:1]) * (1.0 / (NY * NZ * nq))
    inverse2 = kds[y]
    factor = to_col(summed[0:1] * inverse2[2:3])
    for i in range(2):
        low, high = i * (nd // 2), (i + 1) * (nd // 2)
        got(rd.at[:, d_halves[i]], R_GD[i], sib)
        grad = acc[nq + low : nq + high]
        for k in (1, 2, 3):
            grad = grad + rd[k - 1, low:high].astype(F32)
        pre = gain * (grad - dall[y, low:high].astype(F32) * factor[low:high])
        gp[t, nq + low : nq + high] = pre.astype(BF16)
        gather_start(lambda j, i=i: gp.at[j, d_parts[i]], R_PD[i], R_PDS, 0)

    got(rq, R_GQ, sib)
    got(kt.at[pl.ds(0, NT - 1)], R_KT, sib)
    grad = acc[0:nq]
    for i in range(4):
        grad = grad + rq[i].astype(F32)
    factor = kt[z]
    factor = to_col(factor[0:1, 0:nq])
    gp[t, 0:nq] = (gain * (grad - qall[z].astype(F32) * factor)).astype(BF16)
    gather_start(lambda j: gp.at[j, q_rows], R_PQ, R_PQS)

    for i in range(2):
        got(gp.at[pl.ds(0, 3), d_parts[i]], R_PD[i], sib)
        for k in X_ORDER:
            gather_pass(lambda j, i=i: gp.at[j, d_parts[i]], R_PDS, k)
    result = None
    for a in (0, 1):
        if a:
            got(gp.at[pl.ds(0, NX), d_rows], R_PDS, sib)
        for k in (0,) + X_ORDER:
            owner = 2 * ((x + k) % NX) + (c + a) % 2
            term = dot_nn(gp[owner, nq:], wt[4 * a + k])
            result = term if result is None else result + term
    out[nq:] = result.astype(BF16)
    result = None
    for a in (0, 1):
        if a:
            got(gp.at[pl.ds(0, NX), q_rows], R_PQS, sib)
        for k in (0,) + X_ORDER:
            owner = 2 * ((x + k) % NX) + (c + a) % 2
            if k and not a:
                got(gp.at[owner, q_rows], R_PQ + k, at_x(k))
                gather_pass(lambda j: gp.at[j, q_rows], R_PQS, k)
            term = dot_nn(gp[owner, 0:nq], wt[4 * a + k])
            result = term if result is None else result + term
    out[0:nq] = result.astype(BF16)
    for copy in sends:
        copy.wait_send()
    for k, copy in passed:

        @pl.when(parity == k % 2)
        def _(copy=copy):
            copy.wait_send()


def shards(
    query_residual, query_hidden, doc_residual, doc_hidden, down_weight, norm_gain, pos_index, neg_index,
):
    nq, width = query_residual.shape
    nd = doc_residual.shape[0]
    depth = query_hidden.shape[1]
    n = nq + nd
    all_q, all_d = NZ * nq, NY * nd
    hbm = pl.BlockSpec(memory_space=pltpu.HBM)
    vmem = pl.BlockSpec(memory_space=pltpu.VMEM)
    grads, loss = pl.pallas_call(
        functools.partial(kernel, nq, nd),
        out_shape=(pltpu.VMEM((n, depth), BF16), jax.ShapeDtypeStruct((1, 1), F32)),
        in_specs=[hbm] * 8,
        out_specs=(vmem, pl.BlockSpec(memory_space=pltpu.SMEM)),
        scratch_shapes=[
            pltpu.VMEM((NT, 1, width), F32),
            pltpu.VMEM((NZ * NY * nq // 128, 1, 128), jnp.int32),
            pltpu.VMEM((NZ * NY * nq // 128, 1, 128), jnp.int32),
            pltpu.VMEM((n, depth), BF16),
            pltpu.VMEM((n, width), BF16),
            pltpu.VMEM((NT, depth, width), BF16),
            pltpu.VMEM((NT, width, depth), BF16),
            pltpu.VMEM((NX, n, width), BF16),
            pltpu.VMEM((NX, n, width), BF16),
            pltpu.VMEM((NX - 1, n, width), BF16),
            pltpu.VMEM((NX - 1, n, width), BF16),
            pltpu.VMEM((n, width), F32),
            pltpu.VMEM((NZ, nq, width), BF16),
            pltpu.VMEM((NZ, nq, width), BF16),
            pltpu.VMEM((NY, nd, width), BF16),
            pltpu.VMEM((NY, nd, width), BF16),
            pltpu.VMEM((NX - 1, nq, all_d), BF16),
            pltpu.VMEM((NX - 1, nq, all_d), BF16),
            pltpu.VMEM((NX, 8, all_d), F32),
            pltpu.VMEM((NX - 1, 8, all_d), F32),
            pltpu.VMEM((NZ, 8, 128), F32),
            pltpu.VMEM((NT, 8, 128), F32),
            pltpu.VMEM((NT, nq, all_d), F32),
            pltpu.VMEM((NT, nq, all_d), BF16),
            pltpu.VMEM((NT, nq, all_d), BF16),
            pltpu.VMEM((NY, nd, all_q), BF16),
            pltpu.VMEM((NZ - 1, nq, width), BF16),
            pltpu.VMEM((2, nq, width), F32),
            pltpu.VMEM((2, nq, width), BF16),
            pltpu.VMEM((2, nq // 2, width), BF16),
            pltpu.VMEM((4, nq, width), BF16),
            pltpu.VMEM((NY - 1, nd, width), BF16),
            pltpu.VMEM((NY - 1, nd, width), BF16),
            pltpu.VMEM((NZ, 8, 128), F32),
            pltpu.VMEM((NT, 8, 128), F32),
            pltpu.VMEM((NT, 8, all_d), F32),
            pltpu.VMEM((NY, 8, nd), F32),
            pltpu.VMEM((NY, 8, nd), F32),
            pltpu.VMEM((NT, n, width), BF16),
            pltpu.SemaphoreType.DMA((16,)),
            pltpu.SemaphoreType.DMA((1,)),
            pltpu.SemaphoreType.DMA((RID.n,)),
        ],
        compiler_params=pltpu.CompilerParams(
            collective_id=0, has_side_effects=True, vmem_limit_bytes=62 * 2**20
        ),
        name="step",
    )(
        query_residual, query_hidden, doc_residual, doc_hidden, down_weight,
        norm_gain.reshape(NT, 1, width), pos_index.reshape(-1, 1, 128), neg_index.reshape(-1, 1, 128),
    )
    return grads[:nq], grads[nq:], loss.reshape(())


def solution(mesh):
    placed = (
        P("dp", "tensor"),
        P("dp", "tensor"),
        P("dp", "tensor"),
        P("dp", "tensor"),
        P("tensor", None),
        P(),
        P(),
        P(),
    )
    return jax.shard_map(
        shards,
        mesh=mesh,
        in_specs=placed,
        out_specs=(P("dp", "tensor"), P("dp", "tensor"), P()),
        check_vma=False,
    )
```

time: 78.3 us -> 73.3 us (0.936)
  Pallas kernels: 74.6 us -> 69.5 us
    pallas_call x1, Pallas kernels: 74.6 us -> 69.5 us  [shards(): pl.pallas_call(functools.partial(kernel, nq, nd), out_shape=(pltpu.VMEM((...]
where the time goes in v4:
time: 73.3 us; the launch traced here: 73.2 us
  Pallas kernels  69.5 us (95%)
  between operations  2.33 us (3%)
  local copies, waits for them, and re-layouts  1.34 us (2%)
    pallas_call x1, Pallas kernels, shards(): pl.pallas_call(functools.partial(kernel, nq, nd), out_shape=(pltpu.VMEM((...  69.5 us

profile of v4, /device:TPU:1, one launch (start us, length us, event | category | flops | bytes accessed | tf_op | source)
XLA Modules:
  0.0 73.2 jit_solution(10209704970175914430)
XLA Ops:
  0.6 69.5 %step.1 = (bf16[192,768]{1,0:T(8,128)(2,1)S(1)}, f32[1,1]{1,0:T(1,128)}) custom-call(bf16[64,512]{1,0:T(8,128)(2,1)} %q_res.1, bf16[64,768]{1,0:T(8,128)(2,1)} %q_hid.1, bf16[128,512]{1,0:T(8,128)(2,1)} %d_res.1, bf16[128,768]{1,0:T(8,128)(2,1)} %d_hid.1, bf16[768,4096]{1,0:T(8,128)(2,1)} %w_hbm.1, f32[8,1,512]{2,1,0:T(1,128)} %bitcast.4, ...), custom_call_target="tpu_custom_call" | custom-call | tf_op jit(solution)/shard_map/step/pallas_call | solution.py:469
  70.1 0.6 slice.6
  70.8 0.7 slice.7

commit v5 on v4

--- a/solution.py
+++ b/solution.py
@@ -1,4 +1,5 @@
 import functools
+import math
 
 import jax
 import jax.numpy as jnp
@@ -113,7 +114,7 @@
             device_id=device, device_id_type=MESH,
         )
         copy.start()
-        sends.append(copy)
+        sends.append(math.prod(src.shape) * jnp.dtype(src.dtype).itemsize)
 
     def got(dst, rid, device):
         pltpu.make_async_remote_copy(
@@ -136,7 +137,7 @@
     h_loads = [load(q_hid, hid.at[pl.ds(0, nq)]), load(d_hid, hid.at[pl.ds(nq, nd)])]
     x_all = X_ORDER + (0,)
     w_loads = {}
-    width = res.shape[1]
+    depth, width = hid.shape[1], res.shape[1]
     steps = ((1, 2), (1, 1), (0, 2), (1, 3), (0, 1), (1, 0), (0, 3), (0, 0))
     for a, k in steps:
         owner = 2 * ((x + k) % NX) + (c + a) % 2
@@ -169,18 +170,17 @@
         if k:
             s2[k - 1] = part.astype(BF16)
             push(s2.at[k - 1, q_rows], r2.at[3 - k, q_rows], R_XQ, at_x(k))
-            push(s2.at[k - 1, d_parts[0]], r2.at[3 - k, d_parts[0]], R_XD[0], at_x(k))
         else:
             acc[...] = part
         if k == 3:
-            for k in X_ORDER:
-                push(s2.at[k - 1, d_parts[1]], r2.at[3 - k, d_parts[1]], R_XD[1], at_x(k))
+            for place, rid in zip(d_parts, R_XD):
+                for k in X_ORDER:
+                    push(s2.at[k - 1, place], r2.at[3 - k, place], rid, at_x(k))
     for copy in r_loads:
         copy.wait()
     gain = gain_ref[t]
 
     parity = (z + c + 1) % 2
-    passed = []
 
     def pass_q(k):
         slot = (z + k) % NZ
@@ -188,7 +188,6 @@
             src_ref=qall.at[slot], dst_ref=qs.at[slot], send_sem=send.at[0],
             recv_sem=recv.at[R_QS], device_id=sib, device_id_type=MESH,
         )
-        passed.append((k, copy))
 
         @pl.when(parity == k % 2)
         def _():
@@ -257,19 +256,19 @@
             total = total + wide * wide
         return to_row(jnp.sum(total, axis=1, keepdims=True))
 
-    ss_d = jnp.concatenate([squares(dall[k], ds[k]) for k in range(NY)], axis=1)
     got(qs.at[pl.ds(0, NZ // 2)], R_QS, sib)
     owners = [2 * ((x + k) % NX) + c for k in x_all]
-    for k, owner in zip(x_all, owners):
-        s3t[k] = rows8(pad_lanes(squares(qall[owner], qs[owner]), all_d), ss_d)
-        if k:
-            push(s3t.at[k], r3t.at[3 - k], R_SS, at_x(k))
     scores = dot_nt(jnp.concatenate([qall[i] for i in owners], 0), dall[...].reshape(all_d, width))
     scores = scores + dot_nt(jnp.concatenate([qs[i] for i in owners], 0), ds[...].reshape(all_d, width))
     for i, k in enumerate(X_ORDER):
         s3[k - 1] = scores[i * nq : (i + 1) * nq].astype(BF16)
         push(s3.at[k - 1], r3.at[3 - k], R_SX, at_x(k))
     own_scores = scores[3 * nq :]
+    ss_d = jnp.concatenate([squares(dall[k], ds[k]) for k in range(NY)], axis=1)
+    for k, owner in zip(x_all, owners):
+        s3t[k] = rows8(pad_lanes(squares(qall[owner], qs[owner]), all_d), ss_d)
+        if k:
+            push(s3t.at[k], r3t.at[3 - k], R_SS, at_x(k))
     turn(4, 6)
     got(r3t, R_SS, sib)
     tail = s3t[0] + r3t[0] + r3t[1] + r3t[2]
@@ -322,37 +321,63 @@
         push(row.at[t], row.at[t], R_ROW, at_t(k))
     soft = jnp.maximum(margin, 0.0) + jnp.log1p(low)
     loss_part = jnp.sum(jnp.log(tot_row) - pos_row + soft, axis=1, keepdims=True)
-    for k in X_ORDER:
-        got(cf.at[2 * ((x + k) % NX) + c], R_CF + k, at_x(k))
-        gather_pass(lambda i: cf.at[i], R_CS, k)
-    got(row.at[pl.ds(0, NT - 1)], R_ROW, sib)
-    got(cf.at[pl.ds(0, NX)], R_CS, sib)
-    for i in range(NT):
+
+    def make_coef(i):
         factors = row[i]
         coef = cf[i].astype(F32) * to_col(factors[0:1, 0:nq])
         marks = hot[i]
         coef = jnp.where(marks == 1.0, to_col(factors[1:2, 0:nq]) * inv_d, coef)
         coef = jnp.where(marks == 2.0, to_col(factors[2:3, 0:nq]) * inv_d, coef)
-        cg[i] = coef.astype(BF16)
-
-    inner = cg[t].astype(F32) * full
+        return coef.astype(BF16)
+
+    inner = make_coef(t).astype(F32) * full
     kz[z] = rows8(pad_lanes(to_row(jnp.sum(inner, axis=1, keepdims=True)), 128))
     kd[t] = rows8(jnp.sum(inner, axis=0, keepdims=True), jnp.broadcast_to(loss_part, (1, all_d)))
-    for k in Z_ORDER:
-        push(kz.at[z], kz.at[z], R_KZ, at_z(k))
+    to_owner = pltpu.make_async_remote_copy(
+        src_ref=kz.at[z], dst_ref=kz.at[z], send_sem=send.at[1], recv_sem=recv.at[R_KZ],
+        device_id=(y * NZ + t, t), device_id_type=MESH,
+    )
+
+    @pl.when(z != t)
+    def _():
+        to_owner.start()
+
     for k in range(1, NT):
         push(kd.at[t], kd.at[t], R_KD, at_t(k))
+    for k in X_ORDER:
+        got(cf.at[2 * ((x + k) % NX) + c], R_CF + k, at_x(k))
+        gather_pass(lambda i: cf.at[i], R_CS, k)
+    got(row.at[pl.ds(0, NT - 1)], R_ROW, sib)
+    got(kd.at[pl.ds(0, NT - 1)], R_KD, sib)
+    summed = kd[0]
+    for k in range(1, NT):
+        summed = summed + kd[k]
+    summed = rows8(summed[0:1], summed[1:2], inv_d * inv_d)
+    for k in range(NY):
+        kds[k] = summed[:, k * nd : (k + 1) * nd]
+    for k in Y_ORDER:
+        push(kds.at[(y + k) % NY], ky.at[y], R_KY, at_y(k))
+    ky[y] = kds[y]
+    got(cf.at[pl.ds(0, NX)], R_CS, sib)
+    for i in range(NT):
+        cg[i] = make_coef(i)
+
     def grad_q(*offsets):
         rows = [cg[(z + k) % NZ] for k in offsets]
         grad = dot_nn(jnp.concatenate(rows, 0), dall[...].reshape(all_d, width))
         return [grad[i * nq : (i + 1) * nq] for i in range(len(offsets))]
 
-    for i, grad in enumerate(grad_q(3, 5, 4)):
-        sq[i] = grad.astype(BF16)
-    for i, k in enumerate((3, 5)):
-        push(sq.at[i], rq1.at[i], R_G1 + i, at_z(1 if k == 3 else 7))
-    push(sq.at[2, halves[2]], rqh.at[0], R_GH, at_z(2))
-    push(sq.at[2, halves[6]], rqh.at[1], R_GH + 1, at_z(6))
+    def second_stage():
+        for i, k in enumerate((2, 6)):
+            got(rq1.at[i], R_G1 + i, at_z(7 if k == 2 else 1))
+            got(rqh.at[i], R_GH + i, at_z(8 - k))
+            low = slice(0, half) if k == 2 else slice(half, nq)
+            high = slice(half, nq) if k == 2 else slice(0, half)
+            summed = hold[i] + rq1[i].astype(F32)
+            sq[5 + i, low] = (summed[low] + rqh[i].astype(F32)).astype(BF16)
+            sq[5 + i, high] = summed[high].astype(BF16)
+            push(sq.at[5 + i], rq.at[3 - i], R_GQ, at_z(k))
+
     all_q = NZ * nq
     ct[...] = cg[...].reshape(all_q, all_d).T.reshape(NY, nd, all_q)
     rows = jnp.concatenate([ct[(y + k) % NY] for k in Y_ORDER + (0,)], 0)
@@ -364,45 +389,44 @@
     for half_at, rid in zip(d_halves, R_GD):
         for k in Y_ORDER:
             push(sd.at[k - 1, half_at], rd.at[3 - k, half_at], rid, at_y(k))
+    for i, grad in enumerate(grad_q(3, 5, 4)):
+        sq[i] = grad.astype(BF16)
+    for i, k in enumerate((3, 5)):
+        push(sq.at[i], rq1.at[i], R_G1 + i, at_z(1 if k == 3 else 7))
+    push(sq.at[2, halves[2]], rqh.at[0], R_GH, at_z(2))
+    push(sq.at[2, halves[6]], rqh.at[1], R_GH + 1, at_z(6))
+    factor_copies = [
+        pltpu.make_async_remote_copy(
+            src_ref=kt, dst_ref=kt, send_sem=send.at[2], recv_sem=recv.at[R_KT],
+            device_id=at_t(k), device_id_type=MESH,
+        )
+        for k in range(1, NT)
+    ]
+
+    @pl.when(z == t)
+    def _():
+        got(kz.at[pl.ds(0, NZ - 1)], R_KZ, sib)
+        summed = kz[0]
+        for k in range(1, NZ):
+            summed = summed + kz[k]
+        kt[...] = rows8(pad_lanes(summed[0:1, 0:nq] * inv_q_row * inv_q_row, 128))
+        for copy in factor_copies:
+            copy.start()
+
     first, second, third, fourth, own = grad_q(1, 7, 2, 6, 0)
     sq[3], sq[4] = first.astype(BF16), second.astype(BF16)
     for i, k in enumerate((1, 7)):
         push(sq.at[3 + i], rq.at[1 - i], R_GQ, at_z(k))
     hold[0], hold[1] = third, fourth
     acc[0:nq] = own
-    got(kd.at[pl.ds(0, NT - 1)], R_KD, sib)
-    summed = kd[0]
-    for k in range(1, NT):
-        summed = summed + kd[k]
-    summed = rows8(summed[0:1], summed[1:2], inv_d * inv_d)
-    for k in range(NY):
-        kds[k] = summed[:, k * nd : (k + 1) * nd]
-    for k in Y_ORDER:
-        push(kds.at[(y + k) % NY], ky.at[y], R_KY, at_y(k))
-    ky[y] = kds[y]
-    for i, k in enumerate((2, 6)):
-        got(rq1.at[i], R_G1 + i, at_z(7 if k == 2 else 1))
-        got(rqh.at[i], R_GH + i, at_z(8 - k))
-        low = slice(0, half) if k == 2 else slice(half, nq)
-        high = slice(half, nq) if k == 2 else slice(0, half)
-        summed = hold[i] + rq1[i].astype(F32)
-        sq[5 + i, low] = (summed[low] + rqh[i].astype(F32)).astype(BF16)
-        sq[5 + i, high] = summed[high].astype(BF16)
-        push(sq.at[5 + i], rq.at[3 - i], R_GQ, at_z(k))
-    got(kz.at[pl.ds(0, NZ - 1)], R_KZ, sib)
-    summed = kz[0]
-    for k in range(1, NZ):
-        summed = summed + kz[k]
-    kt[t] = rows8(pad_lanes(summed[0:1, 0:nq] * inv_q_row * inv_q_row, 128))
-    for k in range(1, NT):
-        push(kt.at[t], kt.at[t], R_KT, at_t(k))
-
     got(ky.at[pl.ds(0, NY - 1)], R_KY, sib)
     summed = ky[0] + ky[1] + ky[2] + ky[3]
     loss_out[0, 0] = jnp.sum(summed[1:2, 0:1]) * (1.0 / (NY * NZ * nq))
     inverse2 = kds[y]
     factor = to_col(summed[0:1] * inverse2[2:3])
     for i in range(2):
+        if i:
+            second_stage()
         low, high = i * (nd // 2), (i + 1) * (nd // 2)
         got(rd.at[:, d_halves[i]], R_GD[i], sib)
         grad = acc[nq + low : nq + high]
@@ -413,12 +437,14 @@
         gather_start(lambda j, i=i: gp.at[j, d_parts[i]], R_PD[i], R_PDS, 0)
 
     got(rq, R_GQ, sib)
-    got(kt.at[pl.ds(0, NT - 1)], R_KT, sib)
+    @pl.when(z != t)
+    def _():
+        got(kt, R_KT, sib)
+
     grad = acc[0:nq]
     for i in range(4):
         grad = grad + rq[i].astype(F32)
-    factor = kt[z]
-    factor = to_col(factor[0:1, 0:nq])
+    factor = to_col(kt[0:1, 0:nq])
     gp[t, 0:nq] = (gain * (grad - qall[z].astype(F32) * factor)).astype(BF16)
     gather_start(lambda j: gp.at[j, q_rows], R_PQ, R_PQS)
 
@@ -447,13 +473,31 @@
             term = dot_nn(gp[owner, 0:nq], wt[4 * a + k])
             result = term if result is None else result + term
     out[0:nq] = result.astype(BF16)
-    for copy in sends:
-        copy.wait_send()
-    for k, copy in passed:
-
-        @pl.when(parity == k % 2)
-        def _(copy=copy):
+    @pl.when(z != t)
+    def _():
+        to_owner.wait_send()
+
+    @pl.when(z == t)
+    def _():
+        for copy in factor_copies:
             copy.wait_send()
+
+    left = sum(sends) + (NZ // 2) * nq * width * 2
+    views = (
+        (depth * width * 2, NT, lambda n: wv.at[pl.ds(0, n)]),
+        (width * 32, depth // 16, lambda n: wv.at[0, pl.ds(0, 16 * n)]),
+        (4096, 4, lambda n: wv.at[0, pl.ds(0, 16), pl.ds(0, 128 * n)]),
+    )
+    for size, most, view in views:
+        while left >= size:
+            n = min(left // size, most)
+            part = view(n)
+            pltpu.make_async_remote_copy(
+                src_ref=part, dst_ref=part, send_sem=send.at[0], recv_sem=recv.at[0],
+                device_id=sib, device_id_type=MESH,
+            ).wait_send()
+            left -= n * size
+    assert left == 0
 
 
 def shards(
@@ -506,13 +550,13 @@
             pltpu.VMEM((NY - 1, nd, width), BF16),
             pltpu.VMEM((NY - 1, nd, width), BF16),
             pltpu.VMEM((NZ, 8, 128), F32),
-            pltpu.VMEM((NT, 8, 128), F32),
+            pltpu.VMEM((8, 128), F32),
             pltpu.VMEM((NT, 8, all_d), F32),
             pltpu.VMEM((NY, 8, nd), F32),
             pltpu.VMEM((NY, 8, nd), F32),
             pltpu.VMEM((NT, n, width), BF16),
             pltpu.SemaphoreType.DMA((16,)),
-            pltpu.SemaphoreType.DMA((1,)),
+            pltpu.SemaphoreType.DMA((3,)),
             pltpu.SemaphoreType.DMA((RID.n,)),
         ],
         compiler_params=pltpu.CompilerParams(

time: 73.3 us -> 70.3 us (0.959)
  Pallas kernels: 69.5 us -> 66.5 us
    pallas_call x1, Pallas kernels: 69.5 us -> 66.5 us  [shards(): pl.pallas_call(functools.partial(kernel, nq, nd), out_shape=(pltpu.VMEM((...]
where the time goes in v5:
time: 70.3 us; the launch traced here: 70.2 us
  Pallas kernels  66.5 us (95%)
  between operations  2.33 us (3%)
  local copies, waits for them, and re-layouts  1.34 us (2%)
    pallas_call x1, Pallas kernels, shards(): pl.pallas_call(functools.partial(kernel, nq, nd), out_shape=(pltpu.VMEM((...  66.5 us

profile of v5, /device:TPU:1, one launch (start us, length us, event | category | flops | bytes accessed | tf_op | source)
XLA Modules:
  0.0 70.2 jit_solution(2673431704979084365)
XLA Ops:
  0.6 66.5 %step.1 = (bf16[192,768]{1,0:T(8,128)(2,1)S(1)}, f32[1,1]{1,0:T(1,128)}) custom-call(bf16[64,512]{1,0:T(8,128)(2,1)} %q_res.1, bf16[64,768]{1,0:T(8,128)(2,1)} %q_hid.1, bf16[128,512]{1,0:T(8,128)(2,1)} %d_res.1, bf16[128,768]{1,0:T(8,128)(2,1)} %d_hid.1, bf16[768,4096]{1,0:T(8,128)(2,1)} %w_hbm.1, f32[8,1,512]{2,1,0:T(1,128)} %bitcast.4, ...), custom_call_target="tpu_custom_call" | custom-call | tf_op jit(solution)/shard_map/step/pallas_call | solution.py:513
  67.2 0.6 slice.6
  67.8 0.7 slice.7

commit v6 on v5

--- a/solution.py
+++ b/solution.py
@@ -498,6 +498,15 @@
             ).wait_send()
             left -= n * size
     assert left == 0
+
+
+def split(nq, nd, grads, q_out, d_out, sem):
+    d_copy = pltpu.make_async_copy(grads.at[pl.ds(nq, nd)], d_out, sem.at[0])
+    q_copy = pltpu.make_async_copy(grads.at[pl.ds(0, nq)], q_out, sem.at[1])
+    d_copy.start()
+    q_copy.start()
+    d_copy.wait()
+    q_copy.wait()
 
 
 def shards(
@@ -567,7 +576,15 @@
         query_residual, query_hidden, doc_residual, doc_hidden, down_weight,
         norm_gain.reshape(NT, 1, width), pos_index.reshape(-1, 1, 128), neg_index.reshape(-1, 1, 128),
     )
-    return grads[:nq], grads[nq:], loss.reshape(())
+    query_grad, doc_grad = pl.pallas_call(
+        functools.partial(split, nq, nd),
+        out_shape=(jax.ShapeDtypeStruct((nq, depth), BF16), jax.ShapeDtypeStruct((nd, depth), BF16)),
+        in_specs=[vmem],
+        out_specs=(hbm, hbm),
+        scratch_shapes=[pltpu.SemaphoreType.DMA((2,))],
+        name="split",
+    )(grads)
+    return query_grad, doc_grad, loss.reshape(())
 
 
 def solution(mesh):

time: 70.3 us -> 71.4 us (1.016)
  Pallas kernels: 66.5 us -> 68.2 us
    pallas_call x0 -> x1, Pallas kernels: none -> 1.68 us  [shards(): pl.pallas_call(functools.partial(split, nq, nd), out_shape=(jax.ShapeDtyp...]
    slice x2 -> x0, local copies, waits for them, and re-layouts: 1.34 us -> none  [shards(): return (grads[:nq], grads[nq:], loss.reshape(()))]
where the time goes in v6:
time: 71.4 us; the launch traced here: 71.3 us
  Pallas kernels  68.2 us (96%)
  between operations  2.34 us (3%)
    pallas_call x1, Pallas kernels, shards(): pl.pallas_call(functools.partial(kernel, nq, nd), out_shape=(pltpu.VMEM((...  66.5 us
    pallas_call x1, Pallas kernels, shards(): pl.pallas_call(functools.partial(split, nq, nd), out_shape=(jax.ShapeDtyp...  1.68 us

profile of v6, /device:TPU:1, one launch (start us, length us, event | category | flops | bytes accessed | tf_op | source)
XLA Modules:
  0.0 71.3 jit_solution(691654367295122728)
XLA Ops:
  0.6 66.5 %step.1 = (bf16[192,768]{1,0:T(8,128)(2,1)S(1)}, f32[1,1]{1,0:T(1,128)}) custom-call(bf16[64,512]{1,0:T(8,128)(2,1)} %q_res.1, bf16[64,768]{1,0:T(8,128)(2,1)} %q_hid.1, bf16[128,512]{1,0:T(8,128)(2,1)} %d_res.1, bf16[128,768]{1,0:T(8,128)(2,1)} %d_hid.1, bf16[768,4096]{1,0:T(8,128)(2,1)} %w_hbm.1, f32[8,1,512]{2,1,0:T(1,128)} %bitcast.4, ...), custom_call_target="tpu_custom_call" | custom-call | tf_op jit(solution)/shard_map/step/pallas_call | solution.py:522
  67.2 0.0 copy-start
  67.2 0.7 copy-done
  67.9 1.7 %split.1 = (bf16[64,768]{1,0:T(8,128)(2,1)}, bf16[128,768]{1,0:T(8,128)(2,1)}) custom-call(bf16[192,768]{1,0:T(8,128)(2,1)} %copy-done), custom_call_target="tpu_custom_call" | custom-call | tf_op jit(solution)/shard_map/split/pallas_call | solution.py:579
Async XLA Ops:
  67.2 0.7 copy-start
